TPU v7x, 256 devices: a whole 4x4x8 slice. The times are simulated.
256 devices in a mesh: ctx: 64 (over y, z, x_lo), dp: 4 (over x_hi, core).
Axes of the slice: x: 4 (x_hi: 2, x_lo: 2; x = x_hi * 2 + x_lo), y: 4, z: 8, core: 2. Of those that a mesh axis runs over, the one named last changes fastest.
Arguments:
- queries: bfloat16 [65536, 512], P(('dp', 'ctx')), parts along dimension 0, may hold values from -6 to 6
- key_head: bfloat16 [65536, 128], P(('dp', 'ctx')), parts along dimension 0, may hold values from -6 to 6
- value_head: bfloat16 [65536, 128], P(('dp', 'ctx')), parts along dimension 0, may hold values from -6 to 6
- attn_out: bfloat16 [65536, 512], P(('dp', 'ctx')), parts along dimension 0, may hold values from -3 to 3
- out_grads: bfloat16 [65536, 512], P(('dp', 'ctx')), parts along dimension 0, may hold values from -24 to 24
- log_norms: float32 [4, 65536], P(None, ('dp', 'ctx')), parts along dimension 1, may hold values from -1 to 14
- pairing: int32 [256], P('dp'), parts along dimension 0, may hold values from 0 to 63, as said below
Outputs:
- query_grad: float32 [65536, 512], P(('dp', 'ctx')), parts along dimension 0
- key_grad: float32 [65536, 128], P(('dp', 'ctx')), parts along dimension 0
- value_grad: float32 [65536, 128], P(('dp', 'ctx')), parts along dimension 0
There are 4 independent parts, one for each index of `dp`. A program takes and returns all parts, laid end to end along the dimension named above; each array names one. Nothing has to cross between parts.
Inputs may be any that keep to these rules, and one draw needn't show every extreme that they name: pairing is a permutation of 0 to 63.
All inputs are finite; a program needn't handle non-finite values.
Results may differ from a plain program's by a relative error of at most 0.0029.
Values may be sent and summed in bfloat16 or wider, within the bound.
No kernel may reach another device: no remote copies, remote signals or barrier semaphores. Data moves between devices by JAX's collectives and lax.ppermute only.
A program may use at most 128 MiB of HBM per device.

v0:
```python
import math

import jax
import jax.numpy as jnp
from jax import lax
from jax.sharding import PartitionSpec as P


def score_tile(
    query_rows, grad_rows, norm_rows, delta_rows, key_rows, value_rows, weight, score_scale
):
    scores = (
        jnp.einsum("qhd,kd->hqk", query_rows, key_rows, preferred_element_type=jnp.float32)
        * score_scale
    )
    probs = jnp.exp(scores - norm_rows[:, :, None]) * weight
    dprobs = jnp.einsum("qhd,kd->hqk", grad_rows, value_rows, preferred_element_type=jnp.float32)
    dscores = (probs * (dprobs - delta_rows[:, :, None]) * score_scale).astype(jnp.bfloat16)
    probs_low = probs.astype(jnp.bfloat16)
    value_part = jnp.einsum("hqk,qhd->kd", probs_low, grad_rows, preferred_element_type=jnp.float32)
    key_part = jnp.einsum("hqk,qhd->kd", dscores, query_rows, preferred_element_type=jnp.float32)
    query_part = jnp.einsum("hqk,kd->qhd", dscores, key_rows, preferred_element_type=jnp.float32)
    return (query_part, key_part, value_part)


def body(queries, key_head, value_head, attn_out, out_grads, log_norms, pairing):
    row_count, head_dim = key_head.shape
    half_rows = row_count // 2
    head_count = log_norms.shape[0]
    score_scale = 1.0 / math.sqrt(head_dim)
    shard_count = lax.axis_size("ctx")
    self_index = lax.axis_index("ctx")
    query_heads = queries.reshape(row_count, head_count, head_dim)
    grad_heads = out_grads.reshape(row_count, head_count, head_dim)
    deltas = jnp.sum(
        attn_out.reshape(row_count, head_count, head_dim).astype(jnp.float32)
        * grad_heads.astype(jnp.float32),
        axis=2,
    ).T
    shard_range = jnp.arange(shard_count, dtype=jnp.int32)

    def rank_of(index_values):
        return jnp.sum(jnp.where(index_values[..., None] == shard_range, pairing, 0), axis=-1)

    own_rank = rank_of(self_index)
    lower_tri = (jnp.arange(half_rows)[:, None] >= jnp.arange(half_rows)[None, :]).astype(
        jnp.float32
    )
    diag_low = score_tile(
        query_heads[:half_rows],
        grad_heads[:half_rows],
        log_norms[:, :half_rows],
        deltas[:, :half_rows],
        key_head[:half_rows],
        value_head[:half_rows],
        lower_tri,
        score_scale,
    )
    diag_high = score_tile(
        query_heads[half_rows:],
        grad_heads[half_rows:],
        log_norms[:, half_rows:],
        deltas[:, half_rows:],
        key_head[half_rows:],
        value_head[half_rows:],
        lower_tri,
        score_scale,
    )
    batched_tile = jax.vmap(score_tile, in_axes=(0, 0, 0, 0, 0, 0, 0, None))

    def group_work(key_group, value_group, shard_ids):
        group_size = key_group.shape[0]
        low_keys = key_group[:, :half_rows].reshape(group_size * half_rows, head_dim)
        low_values = value_group[:, :half_rows].reshape(group_size * half_rows, head_dim)
        first_query, first_key, first_value = score_tile(
            query_heads[half_rows:],
            grad_heads[half_rows:],
            log_norms[:, half_rows:],
            deltas[:, half_rows:],
            low_keys,
            low_values,
            1.0,
            score_scale,
        )
        is_lower = rank_of(shard_ids) < own_rank
        keep_weight = (shard_ids != self_index).astype(jnp.float32)
        pick_four = is_lower[:, None, None, None]
        pick_three = is_lower[:, None, None]
        sel_queries = jnp.where(
            pick_four, query_heads[None, :half_rows], query_heads[None, half_rows:]
        )
        sel_grads = jnp.where(pick_four, grad_heads[None, :half_rows], grad_heads[None, half_rows:])
        sel_norms = jnp.where(
            pick_three, log_norms[None, :, :half_rows], log_norms[None, :, half_rows:]
        )
        sel_deltas = jnp.where(pick_three, deltas[None, :, :half_rows], deltas[None, :, half_rows:])
        sel_keys = jnp.where(pick_three, key_group[:, :half_rows], key_group[:, half_rows:])
        sel_values = jnp.where(pick_three, value_group[:, :half_rows], value_group[:, half_rows:])
        second_query, second_key, second_value = batched_tile(
            sel_queries,
            sel_grads,
            sel_norms,
            sel_deltas,
            sel_keys,
            sel_values,
            keep_weight,
            score_scale,
        )
        lower_add = jnp.sum(jnp.where(pick_four, second_query, 0.0), axis=0)
        upper_add = first_query + jnp.sum(jnp.where(pick_four, 0.0, second_query), axis=0)
        key_part = jnp.concatenate(
            [
                first_key.reshape(group_size, half_rows, head_dim)
                + jnp.where(pick_three, second_key, 0.0),
                jnp.where(pick_three, 0.0, second_key),
            ],
            axis=1,
        )
        value_part = jnp.concatenate(
            [
                first_value.reshape(group_size, half_rows, head_dim)
                + jnp.where(pick_three, second_value, 0.0),
                jnp.where(pick_three, 0.0, second_value),
            ],
            axis=1,
        )
        return (lower_add, upper_add, key_part, value_part)

    lower_acc = diag_low[0]
    upper_acc = diag_high[0]
    piece_keys = lax.all_gather(key_head, "ctx", axis=0, tiled=True)
    piece_values = lax.all_gather(value_head, "ctx", axis=0, tiled=True)
    piece_shards = piece_keys.shape[0] // row_count
    group_size = math.gcd(piece_shards, 4)
    group_count = piece_shards // group_size
    shard_ids = jnp.arange(piece_shards, dtype=jnp.int32).reshape(group_count, group_size)
    key_groups = piece_keys.reshape(group_count, group_size, row_count, head_dim)
    value_groups = piece_values.reshape(group_count, group_size, row_count, head_dim)

    def scan_step(inner, inputs):
        group_keys, group_values, group_ids = inputs
        lower_add, upper_add, key_part, value_part = group_work(group_keys, group_values, group_ids)
        return ((inner[0] + lower_add, inner[1] + upper_add), (key_part, value_part))

    (lower_acc, upper_acc), (key_parts, value_parts) = lax.scan(
        scan_step, (lower_acc, upper_acc), (key_groups, value_groups, shard_ids)
    )
    key_total = key_parts.reshape(-1, head_dim)
    value_total = value_parts.reshape(-1, head_dim)
    lower_acc, upper_acc, key_total, value_total = (lower_acc, upper_acc, key_total, value_total)
    key_grad, value_grad = (
        lax.psum_scatter(key_total, "ctx", scatter_dimension=0, tiled=True),
        lax.psum_scatter(value_total, "ctx", scatter_dimension=0, tiled=True),
    )
    key_grad = key_grad + jnp.concatenate([diag_low[1], diag_high[1]], axis=0)
    value_grad = value_grad + jnp.concatenate([diag_low[2], diag_high[2]], axis=0)
    query_grad = jnp.concatenate([lower_acc, upper_acc], axis=0).reshape(
        row_count, head_count * head_dim
    )
    return (query_grad, key_grad, value_grad)


def solution(mesh):
    in_specs = (
        P(("dp", "ctx"), None),
        P(("dp", "ctx"), None),
        P(("dp", "ctx"), None),
        P(("dp", "ctx"), None),
        P(("dp", "ctx"), None),
        P(None, ("dp", "ctx")),
        P("dp"),
    )
    out_specs = (P(("dp", "ctx"), None), P(("dp", "ctx"), None), P(("dp", "ctx"), None))
    return jax.shard_map(body, mesh=mesh, in_specs=in_specs, out_specs=out_specs, check_vma=False)
```

profile of v0, /device:TPU:4, one launch (start us, length us, event | category | flops | bytes accessed | tf_op | source)
XLA Modules:
  0.0 1410.5 jit_solution(215568374786599497)
XLA Ops:
  8.7 1.1 copy.79
  9.8 1.1 copy.77
  11.3 1.1 copy.81
  19.9 297.5 %all-gather.5.cloned.1.call-done = bf16[16384,128]{1,0:T(8,128)(2,1)} async-done(((bf16[256,128]{1,0:T(8,128)(2,1)}), bf16[16384,128]{1,0:T(8,128)(2,1)}) %all-gather.5.cloned.1.call-update) | async-done | bytes 4194320 | tf_op jit(solution)/shard_map/all_gather | solution.py:132
  317.4 303.2 %all-gather.3.cloned.1.call-done = bf16[16384,128]{1,0:T(8,128)(2,1)} async-done(((bf16[256,128]{1,0:T(8,128)(2,1)}), bf16[16384,128]{1,0:T(8,128)(2,1)}) %all-gather.3.cloned.1.call-update) | async-done | bytes 4194320 | tf_op jit(solution)/shard_map/all_gather | solution.py:131
  620.6 123.1 %while.17 = (s32[]{:T(128)}, f32[128,4,128]{0,2,1:T(8,128)S(1)}, f32[128,4,128]{0,2,1:T(8,128)S(1)}, f32[16,4,256,128]{3,2,1,0:T(8,128)}, f32[16,4,256,128]{3,2,...) while((s32[]{:T(128)}, f32[128,4,128]{0,2,1:T(8,128)S(1)}, ...), condition=%wide.region_6.7_spmd.clone, body=%wide.region_2.6_spmd.clone.sunk | while | flops 678040320 | bytes 21692452 | solution.py:145
  622.6 1.0 dynamic-slice_bitcast_fusion.5
  627.3 1.1 fusion.174
  635.0 1.1 fusion.174
  638.0 1.0 dynamic-slice_bitcast_fusion.5
  642.7 1.0 fusion.174
  650.4 1.0 fusion.174
  653.3 1.0 dynamic-slice_bitcast_fusion.5
  658.0 1.1 fusion.174
  661.1 1.0 dynamic-slice_bitcast_fusion.5
  665.7 1.1 fusion.174
  673.4 1.0 fusion.174
  676.4 1.0 dynamic-slice_bitcast_fusion.5
  681.1 1.0 fusion.174
  688.8 1.1 fusion.174
  696.5 1.1 fusion.174
  704.2 1.0 fusion.174
  711.9 1.0 fusion.174
  719.6 1.1 fusion.174
  727.3 1.1 fusion.174
  735.0 1.0 fusion.174
  742.6 1.0 fusion.174
  745.1 1.0 copy.117
  746.1 327.3 %reduce-scatter.5.cloned.1.call-done = f32[256,128]{1,0:T(8,128)} async-done(((f32[16384,128]{1,0:T(8,128)}), f32[256,128]{1,0:T(8,128)}) %reduce-scatter.5.cloned.1.call-update) | async-done | bytes 131088 | tf_op jit(solution)/shard_map/reduce_scatter | solution.py:153
  1073.4 1.6 maximum_add_fusion.1
  1075.0 327.4 %reduce-scatter.3.cloned.1.call-done = f32[256,128]{1,0:T(8,128)} async-done(((f32[16384,128]{1,0:T(8,128)}), f32[256,128]{1,0:T(8,128)}) %reduce-scatter.3.cloned.1.call-update) | async-done | bytes 131088 | tf_op jit(solution)/shard_map/reduce_scatter | solution.py:152
  1402.4 1.6 maximum_add_fusion
  (400 shorter events, 109.7 us)
Async XLA Ops:
  7.2 613.5 %copy-start = (f32[4,256]{1,0:T(4,128)S(1)}, f32[4,256]{1,0:T(4,128)}, u32[]{:S(2)}) copy-start(f32[4,256]{1,0:T(4,128)} %param.14) | copy-start | bytes 12292
  7.2 12.1 copy-start.1
  7.2 310.2 %all-gather.5.cloned.1.call-start = ((), (), s32[]{:S(2)}) async-start(), calls=%async_computation.3 | async-start | bytes 4259840 | tf_op jit(solution)/shard_map/all_gather | solution.py:132
  7.9 612.7 %all-gather.3.cloned.1.call-start = ((), (), s32[]{:S(2)}) async-start(), calls=%async_computation.2 | async-start | bytes 4259840 | tf_op jit(solution)/shard_map/all_gather | solution.py:131
  8.7 1064.7 %reduce-scatter.5.cloned.1.call-start = ((), (), s32[]{:S(2)}) async-start(), calls=%async_computation.5 | async-start | bytes 8519680 | tf_op jit(solution)/shard_map/reduce_scatter | solution.py:153
  743.7 658.7 %reduce-scatter.3.cloned.1.call-start = ((), (), s32[]{:S(2)}) async-start(), calls=%async_computation.4 | async-start | bytes 8519680 | tf_op jit(solution)/shard_map/reduce_scatter | solution.py:152
Sparse Core Ops, SparseCore 0:
  9.8 307.5 all-gather.4
  319.2 301.3 all-gather.2
  743.8 329.5 reduce-scatter.4
  1075.8 326.5 reduce-scatter.2
where the time goes:
time: 1410 us
  waiting for transfers between devices  1260 us (89%)
  matrix products  62.6 us (4%)
  local copies, waits for them, and re-layouts  37.8 us (3%)
  other arithmetic  36.4 us (3%)
    reduce_scatter x1, waiting for transfers between devices, body(): lax.psum_scatter(key_total, 'ctx', scatter_dimension=0, tiled=True)  327 us
    reduce_scatter x1, waiting for transfers between devices, body(): lax.psum_scatter(value_total, 'ctx', scatter_dimension=0, tiled=True)  327 us
    all_gather x1, waiting for transfers between devices, body(): piece_keys = lax.all_gather(key_head, 'ctx', axis=0, tiled=True)  303 us
    all_gather x1, waiting for transfers between devices, body(): piece_values = lax.all_gather(value_head, 'ctx', axis=0, tiled=True)  298 us
    squeeze x32, local copies, waits for them, and re-layouts, body(): lax.scan(scan_step, (lower_acc, upper_acc), (key_groups, value_groups, sh...  31.1 us
  transfers between devices with their start and end apart: 4, of which 4 were waited for; matrix products, arithmetic and copies ran while one was open for 1% of the time, Pallas kernels for 0%

commit v1 on v0

v1 whole, which is shorter than its diff:
```python
import math

import jax
import jax.numpy as jnp
from jax import lax
from jax.experimental import pallas as pl
from jax.experimental.pallas import tpu as pltpu
from jax.sharding import PartitionSpec as P

F32 = jnp.float32
BF16 = jnp.bfloat16
HEAD = 128
HEADS = 4
HALF = 128
ROWS = HEADS * HALF
NY, NZ, NX = 4, 8, 2
SCALE = 1.0 / math.sqrt(HEAD)
LOG2E = math.log2(math.e)
NT = (((1,), (1,)), ((), ()))
TN = (((0,), (0,)), ((), ()))
CHUNK = 4


def dot(a, b, dims):
    return lax.dot_general(a, b, dims, preferred_element_type=F32)


def attention_kernel(n_q, n_k, *refs):
    rq, rk = refs[:2]
    q_refs = refs[2 : 2 + n_q]
    g_refs = refs[2 + n_q : 2 + 2 * n_q]
    st_refs = refs[2 + 2 * n_q : 2 + 3 * n_q]
    at = 2 + 3 * n_q
    kv_refs = refs[at : at + n_k]
    own_dq, far_dq, own_dkv, far_dkv = refs[at + n_k : at + n_k + 4]
    qs, gs, ns, ds, ks, vs, dks, dvs, acc = refs[at + n_k + 4 :]
    for d in range(n_q):
        for half in range(2):
            i = 2 * d + half
            rows = slice(half * HALF, (half + 1) * HALF)
            for h in range(HEADS):
                cols = slice(h * HEAD, (h + 1) * HEAD)
                qs[i, cols, :] = q_refs[d][rows, cols]
                gs[i, cols, :] = g_refs[d][rows, cols]
                ns[i, :, cols] = st_refs[d][h : h + 1, rows] * LOG2E
                ds[i, :, cols] = st_refs[d][HEADS + h : HEADS + h + 1, rows]
    for e in range(n_k):
        for half in range(2):
            rows = slice(half * HALF, (half + 1) * HALF)
            ks[half, e * HALF : (e + 1) * HALF, :] = kv_refs[e][rows, :HEAD]
            vs[half, e * HALF : (e + 1) * HALF, :] = kv_refs[e][rows, HEAD:]
    acc[...] = jnp.zeros_like(acc)

    def tile(i, k, v, keep=None):
        q, g = qs[i], gs[i]
        scores = dot(k, q, NT)
        probs = jnp.exp2(scores * (SCALE * LOG2E) - ns[i])
        if keep is not None:
            probs = jnp.where(keep, probs, 0.0)
        dprobs = dot(v, g, NT)
        dscores = (probs * (dprobs - ds[i]) * SCALE).astype(BF16)
        probs_low = probs.astype(BF16)
        dv = jnp.dot(probs_low, g, preferred_element_type=F32)
        dk = jnp.dot(dscores, q, preferred_element_type=F32)
        acc[i] += dot(k, dscores, TN)
        return dk, dv

    def first(c, carry):
        keys = pl.ds(pl.multiple_of(c * (CHUNK * HALF), CHUNK * HALF), CHUNK * HALF)
        k, v = ks[0, keys, :], vs[0, keys, :]
        dk = dv = 0.0
        for d in range(n_q):
            x, y = tile(2 * d + 1, k, v)
            dk, dv = dk + x, dv + y
        dks[0, keys, :] = dk
        dvs[0, keys, :] = dv
        dks[1, keys, :] = jnp.zeros_like(dk)
        dvs[1, keys, :] = jnp.zeros_like(dv)
        return carry

    lax.fori_loop(0, n_k // CHUNK, first, 0)

    def second(e, d):
        half = jnp.where(rk[e] < rq[d], 0, 1)
        keys = pl.ds(pl.multiple_of(e * HALF, HALF), HALF)
        x, y = tile(2 * d + half, ks[half, keys, :], vs[half, keys, :])
        dks[half, keys, :] += x
        dvs[half, keys, :] += y

    def second_all(e, carry):
        for d in range(n_q):
            second(e, d)
        return carry

    lax.fori_loop(1, n_k, second_all, 0)
    for d in range(1, n_q):
        second(0, d)
    key_at = lax.broadcasted_iota(jnp.int32, (HALF, ROWS), 0)
    row_at = lax.broadcasted_iota(jnp.int32, (HALF, ROWS), 1) & (HALF - 1)
    keep = row_at >= key_at
    for half in range(2):
        x, y = tile(half, ks[half, :HALF, :], vs[half, :HALF, :], keep)
        dks[half, :HALF, :] += x
        dvs[half, :HALF, :] += y
    for d in range(n_q):
        for half in range(2):
            rows = slice(half * HALF, (half + 1) * HALF)
            for h in range(HEADS):
                cols = slice(h * HEAD, (h + 1) * HEAD)
                block = acc[2 * d + half, :, cols].T
                if d == 0:
                    own_dq[rows, cols] = block
                else:
                    far_dq[d - 1, rows, cols] = block.astype(BF16)
    for e in range(n_k):
        keys = slice(e * HALF, (e + 1) * HALF)
        for half in range(2):
            rows = slice(half * HALF, (half + 1) * HALF)
            if e % 2 == 0:
                own_dkv[e // 2, rows, :HEAD] = dks[half, keys, :]
                own_dkv[e // 2, rows, HEAD:] = dvs[half, keys, :]
            else:
                far_dkv[e // 2, rows, :HEAD] = dks[half, keys, :].astype(BF16)
                far_dkv[e // 2, rows, HEAD:] = dvs[half, keys, :].astype(BF16)


def attention(rq, rk, queries, grads, stats, kvs):
    n_q, n_k = len(queries), len(kvs)
    pairs = n_q * n_k
    smem = pl.BlockSpec(memory_space=pltpu.SMEM)
    vmem = pl.BlockSpec(memory_space=pltpu.VMEM)

    def kernel(*refs):
        attention_kernel(n_q, n_k, *refs)

    return pl.pallas_call(
        kernel,
        out_shape=(
            jax.ShapeDtypeStruct((2 * HALF, ROWS), F32),
            jax.ShapeDtypeStruct((n_q - 1, 2 * HALF, ROWS), BF16),
            jax.ShapeDtypeStruct((n_k // 2, 2 * HALF, 2 * HEAD), F32),
            jax.ShapeDtypeStruct((n_k // 2, 2 * HALF, 2 * HEAD), BF16),
        ),
        in_specs=[smem, smem] + [vmem] * (3 * n_q + n_k),
        out_specs=(vmem,) * 4,
        scratch_shapes=[
            pltpu.VMEM((2 * n_q, ROWS, HEAD), BF16),
            pltpu.VMEM((2 * n_q, ROWS, HEAD), BF16),
            pltpu.VMEM((2 * n_q, 1, ROWS), F32),
            pltpu.VMEM((2 * n_q, 1, ROWS), F32),
            pltpu.VMEM((2, n_k * HALF, HEAD), BF16),
            pltpu.VMEM((2, n_k * HALF, HEAD), BF16),
            pltpu.VMEM((2, n_k * HALF, HEAD), F32),
            pltpu.VMEM((2, n_k * HALF, HEAD), F32),
            pltpu.VMEM((2 * n_q, HEAD, ROWS), F32),
        ],
        compiler_params=pltpu.CompilerParams(vmem_limit_bytes=44 * 1024 * 1024),
        cost_estimate=pl.CostEstimate(
            flops=pairs * 2 * 5 * 2 * HALF * HALF * ROWS,
            bytes_accessed=8 * 1024 * 1024,
            transcendentals=pairs * 2 * HALF * ROWS,
        ),
    )(rq, rk, *queries, *grads, *stats, *kvs)


def index_of(y, z, x):
    return (y * NZ + z) * NX + x


def shift(dy, dz, flip):
    return [
        (index_of((y + dy) % NY, (z + dz) % NZ, x ^ flip), index_of(y, z, x))
        for y in range(NY)
        for z in range(NZ)
        for x in range(NX)
    ]


def fetch(array, dy=0, dz=0, flip=0):
    return lax.ppermute(array, "ctx", shift(dy % NY, dz % NZ, flip))


def body(queries, key_head, value_head, attn_out, out_grads, log_norms, pairing):
    me = lax.axis_index("ctx")
    x, z, y = me % NX, (me // NX) % NZ, me // (NX * NZ)
    shards = jnp.arange(NY * NZ * NX, dtype=jnp.int32)

    def rank_of(index):
        return jnp.sum(jnp.where(index[:, None] == shards, pairing, 0), axis=-1)

    q_at = index_of((y + jnp.arange(NY)) % NY, z, x)
    k_slot = jnp.arange(NZ * NX)
    k_at = index_of(y, (z + k_slot // NX) % NZ, x ^ (k_slot % NX))
    rq, rk = rank_of(q_at), rank_of(k_at)

    kv = jnp.concatenate([key_head, value_head], axis=1)
    near = [kv] + [fetch(kv, dz=r) for r in range(1, NZ)]
    kvs = []
    for block in near:
        kvs += [block, fetch(block, flip=1)]
    deltas = jnp.sum(
        (attn_out.astype(F32) * out_grads.astype(F32)).reshape(2 * HALF, HEADS, HEAD), axis=2
    )
    stat = jnp.concatenate([log_norms, deltas.T], axis=0)
    qs = [queries] + [fetch(queries, dy=r) for r in range(1, NY)]
    gs = [out_grads] + [fetch(out_grads, dy=r) for r in range(1, NY)]
    stats = [stat] + [fetch(stat, dy=r) for r in range(1, NY)]

    own_dq, far_dq, own_dkv, far_dkv = attention(rq, rk, qs, gs, stats, kvs)

    other = fetch(far_dkv, flip=1)
    dq = own_dq
    for r in range(1, NY):
        dq = dq + fetch(far_dq[r - 1], dy=-r).astype(F32)
    mixed = own_dkv + other.astype(F32)
    dkv = mixed[0]
    for r in range(1, NZ):
        dkv = dkv + fetch(mixed[r].astype(BF16), dz=-r).astype(F32)
    return dq, dkv[:, :HEAD], dkv[:, HEAD:]


def solution(mesh):
    rows = P(("dp", "ctx"), None)
    in_specs = (rows,) * 5 + (P(None, ("dp", "ctx")), P("dp"))
    return jax.shard_map(
        body, mesh=mesh, in_specs=in_specs, out_specs=(rows,) * 3, check_vma=False
    )
```

time: 1410 us -> 161 us (0.11)
  waiting for transfers between devices: 1260 us -> 60.2 us
  matrix products: 62.6 us -> 0 us
  starting transfers between devices: 0.16 us -> 58.9 us
  local copies, waits for them, and re-layouts: 37.8 us -> 2.87 us
  other arithmetic: 36.4 us -> 3.22 us
  Pallas kernels: 0 us -> 32.4 us
    reduce_scatter x2 -> x0, waiting for transfers between devices: 655 us -> none  [the longest x1 327 us: body(): lax.psum_scatter(key_total, 'ctx', scatter_dimension=0, tiled=True)]
    all_gather x2 -> x0, waiting for transfers between devices: 601 us -> none  [the longest x1 303 us: body(): piece_keys = lax.all_gather(key_head, 'ctx', axis=0, tiled=True)]
    dot_general x170 -> x0, matrix products: 62.6 us -> none  [the longest x34 13.9 us: score_tile(): jnp.einsum('hqk,kd->qhd', dscores, key_rows, preferred_element_type=jnp.f...]
    ppermute x0 -> x35, waiting for transfers between devices: none -> 60.2 us  [fetch(): return lax.ppermute(array, 'ctx', shift(dy % NY, dz % NZ, flip))]
    ppermute x0 -> x35, starting transfers between devices: none -> 58.9 us  [fetch(): return lax.ppermute(array, 'ctx', shift(dy % NY, dz % NZ, flip))]
    pallas_call x0 -> x1, Pallas kernels: none -> 32.4 us  [attention(): pl.pallas_call(kernel, out_shape=(jax.ShapeDtypeStruct((2 * HALF, ROWS),...]
    squeeze x32 -> x1, local copies, waits for them, and re-layouts: 31.1 us -> 0.05 us  [body(): dq = dq + fetch(far_dq[r - 1], dy=-r).astype(F32)]
    dynamic_update_slice x16 -> x0, other arithmetic: 16.9 us -> none  [body(): lax.scan(scan_step, (lower_acc, upper_acc), (key_groups, value_groups, sh...]
  transfers between devices with their start and end apart: 4 -> 35, of which waited for: 4 -> 15; matrix products, arithmetic and copies ran while one was open for 1% -> 2% of each run, Pallas kernels for 0% -> 0%
where the time goes in v1:
time: 161 us; the launch traced here: 158 us
  waiting for transfers between devices  60.2 us (37%)
  starting transfers between devices  58.9 us (37%)
  Pallas kernels  32.4 us (20%)
  other arithmetic  3.22 us (2%)
  local copies, waits for them, and re-layouts  2.87 us (2%)
    ppermute x35, waiting for transfers between devices, fetch(): return lax.ppermute(array, 'ctx', shift(dy % NY, dz % NZ, flip))  60.2 us
    ppermute x35, starting transfers between devices, fetch(): return lax.ppermute(array, 'ctx', shift(dy % NY, dz % NZ, flip))  58.9 us
    pallas_call x1, Pallas kernels, attention(): pl.pallas_call(kernel, out_shape=(jax.ShapeDtypeStruct((2 * HALF, ROWS),...  32.4 us
  transfers between devices with their start and end apart: 35, of which 15 were waited for; matrix products, arithmetic and copies ran while one was open for 2% of the time, Pallas kernels for 0%

profile of v1, /device:TPU:4, one launch (start us, length us, event | category | flops | bytes accessed | tf_op | source)
XLA Modules:
  0.0 158.3 jit_solution(16535244119962001398)
XLA Ops:
  2.4 2.0 %collective-permute-start.22 = (bf16[256,256]{1,0:T(8,128)(2,1)S(1)}, bf16[256,256]{1,0:T(8,128)(2,1)S(1)}, u32[]{:S(2)}, u32[]{:S(2)}) collective-permute-start(bf16[256,256]{1,0:T(8,128)(2,1)S(1)} %constant_dynamic-update-slice_fusion.refs_14_), channel_id=1, source_target_pairs={{56,0},{60,4},{0,8},{4,12},{8,16},{12,20},{16,24},{20,28},{24,32},... | collective-permute-start | bytes 393224 | tf_op jit(solution)/shard_map/ppermute | solution.py:180
  4.4 3.3 %collective-permute-start.20 = (bf16[256,256]{1,0:T(8,128)(2,1)S(1)}, bf16[256,256]{1,0:T(8,128)(2,1)S(1)}, u32[]{:S(2)}, u32[]{:S(2)}) collective-permute-start(bf16[256,256]{1,0:T(8,128)(2,1)S(1)} %constant_dynamic-update-slice_fusion.refs_14_), channel_id=1, source_target_pairs={{48,0},{52,4},{56,8},{60,12},{0,16},{4,20},{8,24},{12,28},{16,32},... | collective-permute-start | bytes 393224 | tf_op jit(solution)/shard_map/ppermute | solution.py:180
  9.5 1.7 %collective-permute-start.8 = (f32[8,256]{1,0:T(8,128)S(1)}, f32[8,256]{1,0:T(8,128)S(1)}, u32[]{:S(2)}, u32[]{:S(2)}) collective-permute-start(f32[8,256]{1,0:T(8,128)S(1)} %pad_maximum_fusion.refs_10_), channel_id=1, source_target_pairs={{192,0},{196,4},{200,8},{204,12},{208,16},{212,20},{216,24},{220,2... | collective-permute-start | bytes 24584 | tf_op jit(solution)/shard_map/ppermute | solution.py:180
  11.1 2.9 %collective-permute-start.7 = (f32[8,256]{1,0:T(8,128)S(1)}, f32[8,256]{1,0:T(8,128)S(1)}, u32[]{:S(2)}, u32[]{:S(2)}) collective-permute-start(f32[8,256]{1,0:T(8,128)S(1)} %pad_maximum_fusion.refs_10_), channel_id=1, source_target_pairs={{128,0},{132,4},{136,8},{140,12},{144,16},{148,20},{152,24},{156,2... | collective-permute-start | bytes 24584 | tf_op jit(solution)/shard_map/ppermute | solution.py:180
  14.0 1.3 collective-permute-start.6
  15.4 4.0 %collective-permute-start.18 = (bf16[256,256]{1,0:T(8,128)(2,1)S(1)}, bf16[256,256]{1,0:T(8,128)(2,1)S(1)}, u32[]{:S(2)}, u32[]{:S(2)}) collective-permute-start(bf16[256,256]{1,0:T(8,128)(2,1)S(1)} %constant_dynamic-update-slice_fusion.refs_14_), channel_id=1, source_target_pairs={{40,0},{44,4},{48,8},{52,12},{56,16},{60,20},{0,24},{4,28},{8,32},... | collective-permute-start | bytes 393224 | tf_op jit(solution)/shard_map/ppermute | solution.py:180
  19.4 1.4 collective-permute-start.16
  20.8 4.1 %collective-permute-start.14 = (bf16[256,256]{1,0:T(8,128)(2,1)S(1)}, bf16[256,256]{1,0:T(8,128)(2,1)S(1)}, u32[]{:S(2)}, u32[]{:S(2)}) collective-permute-start(bf16[256,256]{1,0:T(8,128)(2,1)S(1)} %constant_dynamic-update-slice_fusion.refs_14_), channel_id=1, source_target_pairs={{24,0},{28,4},{32,8},{36,12},{40,16},{44,20},{48,24},{52,28},{56,3... | collective-permute-start | bytes 393224 | tf_op jit(solution)/shard_map/ppermute | solution.py:180
  24.9 2.7 %collective-permute-start.12 = (bf16[256,256]{1,0:T(8,128)(2,1)S(1)}, bf16[256,256]{1,0:T(8,128)(2,1)S(1)}, u32[]{:S(2)}, u32[]{:S(2)}) collective-permute-start(bf16[256,256]{1,0:T(8,128)(2,1)S(1)} %constant_dynamic-update-slice_fusion.refs_14_), channel_id=1, source_target_pairs={{16,0},{20,4},{24,8},{28,12},{32,16},{36,20},{40,24},{44,28},{48,3... | collective-permute-start | bytes 393224 | tf_op jit(solution)/shard_map/ppermute | solution.py:180
  28.6 1.8 %collective-permute-done.18.refs_24_ = bf16[256,256]{1,0:T(8,128)(2,1)S(1)} collective-permute-done((bf16[256,256]{1,0:T(8,128)(2,1)S(1)}, bf16[256,256]{1,0:T(8,128)(2,1)S(1)}, u32[]{:S(2)}, u32[]{:S(2)}) %collective-permute-start.18) | collective-permute-done | bytes 131104 | tf_op jit(solution)/shard_map/ppermute | solution.py:180
  30.3 1.2 collective-permute-start.9
  32.5 8.1 %collective-permute-done.14.refs_20_ = bf16[256,256]{1,0:T(8,128)(2,1)S(1)} collective-permute-done((bf16[256,256]{1,0:T(8,128)(2,1)S(1)}, bf16[256,256]{1,0:T(8,128)(2,1)S(1)}, u32[]{:S(2)}, u32[]{:S(2)}) %collective-permute-start.14) | collective-permute-done | bytes 131104 | tf_op jit(solution)/shard_map/ppermute | solution.py:180
  40.6 1.2 collective-permute-start.21
  45.4 1.2 collective-permute-start.17
  47.4 1.2 collective-permute-start.13
  50.6 1.6 %collective-permute-done.17.refs_23_ = bf16[256,256]{1,0:T(8,128)(2,1)S(1)} collective-permute-done((bf16[256,256]{1,0:T(8,128)(2,1)S(1)}, bf16[256,256]{1,0:T(8,128)(2,1)S(1)}, u32[]{:S(2)}, u32[]{:S(2)}) %collective-permute-start.17) | collective-permute-done | bytes 131104 | tf_op jit(solution)/shard_map/ppermute | solution.py:180
  52.1 2.2 %collective-permute-start = (bf16[256,512]{1,0:T(8,128)(2,1)S(1)}, bf16[256,512]{1,0:T(8,128)(2,1)S(1)}, u32[]{:S(2)}, u32[]{:S(2)}) collective-permute-start(bf16[256,512]{1,0:T(8,128)(2,1)S(1)} %copy-done.1), channel_id=1, source_target_pairs={{64,0},{68,4},{72,8},{76,12},{80,16},{84,20},{88,24},{92,28},{96,3... | collective-permute-start | bytes 786440 | tf_op jit(solution)/shard_map/ppermute | solution.py:180
  55.3 2.5 %collective-permute-done.13.refs_19_ = bf16[256,256]{1,0:T(8,128)(2,1)S(1)} collective-permute-done((bf16[256,256]{1,0:T(8,128)(2,1)S(1)}, bf16[256,256]{1,0:T(8,128)(2,1)S(1)}, u32[]{:S(2)}, u32[]{:S(2)}) %collective-permute-start.13) | collective-permute-done | bytes 131104 | tf_op jit(solution)/shard_map/ppermute | solution.py:180
  58.1 1.5 collective-permute-done.11.refs_17_
  60.6 1.9 %collective-permute-start.3 = (bf16[256,512]{1,0:T(8,128)(2,1)S(1)}, bf16[256,512]{1,0:T(8,128)(2,1)S(1)}, u32[]{:S(2)}, u32[]{:S(2)}) collective-permute-start(bf16[256,512]{1,0:T(8,128)(2,1)S(1)} %copy-done), channel_id=1, source_target_pairs={{64,0},{68,4},{72,8},{76,12},{80,16},{84,20},{88,24},{92,28},{96,3... | collective-permute-start | bytes 786440 | tf_op jit(solution)/shard_map/ppermute | solution.py:180
  62.9 5.0 %collective-permute-done.2.refs_5_ = bf16[256,512]{1,0:T(8,128)(2,1)S(1)} collective-permute-done((bf16[256,512]{1,0:T(8,128)(2,1)S(1)}, bf16[256,512]{1,0:T(8,128)(2,1)S(1)}, u32[]{:S(2)}, u32[]{:S(2)}) %collective-permute-start.2) | collective-permute-done | bytes 262176 | tf_op jit(solution)/shard_map/ppermute | solution.py:180
  67.8 6.0 %collective-permute-done.5.refs_9_ = bf16[256,512]{1,0:T(8,128)(2,1)S(1)} collective-permute-done((bf16[256,512]{1,0:T(8,128)(2,1)S(1)}, bf16[256,512]{1,0:T(8,128)(2,1)S(1)}, u32[]{:S(2)}, u32[]{:S(2)}) %collective-permute-start.5) | collective-permute-done | bytes 262176 | tf_op jit(solution)/shard_map/ppermute | solution.py:180
  73.9 32.4 %shard_map.94 = (f32[256,512]{1,0:T(8,128)S(1)}, bf16[3,256,512]{2,1,0:T(8,128)(2,1)S(1)}, f32[8,256,256]{2,1,0:T(8,128)S(1)}, bf16[8,256,256]{2,1,0:T(8,128)(2,1)S(1)}) custom-call(s32[4]{0:T(128)S(1)} %select_reduce_fusion.1.refs_0_, s32[16]{0:T(128)S(1)} %select_reduce_fusion.refs_1_, bf16[256,512]{1,0:T(8,128)(2,1)S(1)} %copy-done.1, ...), custom_call_target="tpu_custom_call" | custom-call | flops 10737418240 | bytes 8388608 | tf_op jit(solution)/shard_map/pallas_call | solution.py:136
  106.3 1.3 collective-permute-start.27
  107.9 3.0 %collective-permute-start.26 = (bf16[256,512]{1,0:T(8,128)(2,1)S(1)}, bf16[256,512]{1,0:T(8,128)(2,1)S(1)}, u32[]{:S(2)}, u32[]{:S(2)}) collective-permute-start(bf16[256,512]{1,0:T(8,128)(2,1)S(1)} %get-tuple-element.21), channel_id=1, source_target_pairs={{64,0},{68,4},{72,8},{76,12},{80,16},{84,20},{88,24},{92,28},{96,3... | collective-permute-start | bytes 786440 | tf_op jit(solution)/shard_map/ppermute | solution.py:180
  110.9 16.5 %collective-permute-done.27 = bf16[8,256,256]{2,1,0:T(8,128)(2,1)S(1)} collective-permute-done((bf16[8,256,256]{2,1,0:T(8,128)(2,1)S(1)}, bf16[8,256,256]{2,1,0:T(8,128)(2,1)S(1)}, u32[]{:S(2)}, u32[]{:S(2)}) %collective-permute-start.27) | collective-permute-done | bytes 1048608 | tf_op jit(solution)/shard_map/ppermute | solution.py:180
  127.8 4.3 %collective-permute-start.28 = (bf16[256,256]{1,0:T(8,128)(2,1)S(1)}, bf16[256,256]{1,0:T(8,128)(2,1)S(1)}, u32[]{:S(2)}, u32[]{:S(2)}) collective-permute-start(bf16[256,256]{1,0:T(8,128)(2,1)S(1)} %get-tuple-element.13), channel_id=1, source_target_pairs={{56,0},{60,4},{0,8},{4,12},{8,16},{12,20},{16,24},{20,28},{24,32},... | collective-permute-start | bytes 393224 | tf_op jit(solution)/shard_map/ppermute | solution.py:180
  132.7 1.4 collective-permute-start.33
  134.1 1.2 collective-permute-start.32
  135.3 5.3 %collective-permute-start.31 = (bf16[256,256]{1,0:T(8,128)(2,1)S(1)}, bf16[256,256]{1,0:T(8,128)(2,1)S(1)}, u32[]{:S(2)}, u32[]{:S(2)}) collective-permute-start(bf16[256,256]{1,0:T(8,128)(2,1)S(1)} %get-tuple-element.17), channel_id=1, source_target_pairs={{32,0},{36,4},{40,8},{44,12},{48,16},{52,20},{56,24},{60,28},{0,32... | collective-permute-start | bytes 393224 | tf_op jit(solution)/shard_map/ppermute | solution.py:180
  143.5 9.7 %collective-permute-done.32 = bf16[256,256]{1,0:T(8,128)(2,1)S(1)} collective-permute-done((bf16[256,256]{1,0:T(8,128)(2,1)S(1)}, bf16[256,256]{1,0:T(8,128)(2,1)S(1)}, u32[]{:S(2)}, u32[]{:S(2)}) %collective-permute-start.32) | collective-permute-done | bytes 131104 | tf_op jit(solution)/shard_map/ppermute | solution.py:180
  153.2 4.2 %collective-permute-done.30 = bf16[256,256]{1,0:T(8,128)(2,1)S(1)} collective-permute-done((bf16[256,256]{1,0:T(8,128)(2,1)S(1)}, bf16[256,256]{1,0:T(8,128)(2,1)S(1)}, u32[]{:S(2)}, u32[]{:S(2)}) %collective-permute-start.30) | collective-permute-done | bytes 131104 | tf_op jit(solution)/shard_map/ppermute | solution.py:180
  (64 shorter events, 19.7 us)
Async XLA Ops:
  2.4 22.5 %collective-permute-start.22 = (bf16[256,256]{1,0:T(8,128)(2,1)S(1)}, bf16[256,256]{1,0:T(8,128)(2,1)S(1)}, u32[]{:S(2)}, u32[]{:S(2)}) collective-permute-start(bf16[256,256]{1,0:T(8,128)(2,1)S(1)} %constant_dynamic-update-slice_fusion.refs_14_), channel_id=1, source_target_pairs={{56,0},{60,4},{0,8},{4,12},{8,16},{12,20},{16,24},{20,28},{24,32},... | collective-permute-start | bytes 393224 | tf_op jit(solution)/shard_map/ppermute | solution.py:180
  4.4 23.1 %collective-permute-start.20 = (bf16[256,256]{1,0:T(8,128)(2,1)S(1)}, bf16[256,256]{1,0:T(8,128)(2,1)S(1)}, u32[]{:S(2)}, u32[]{:S(2)}) collective-permute-start(bf16[256,256]{1,0:T(8,128)(2,1)S(1)} %constant_dynamic-update-slice_fusion.refs_14_), channel_id=1, source_target_pairs={{48,0},{52,4},{56,8},{60,12},{0,16},{4,20},{8,24},{12,28},{16,32},... | collective-permute-start | bytes 393224 | tf_op jit(solution)/shard_map/ppermute | solution.py:180
  11.1 8.3 %collective-permute-start.7 = (f32[8,256]{1,0:T(8,128)S(1)}, f32[8,256]{1,0:T(8,128)S(1)}, u32[]{:S(2)}, u32[]{:S(2)}) collective-permute-start(f32[8,256]{1,0:T(8,128)S(1)} %pad_maximum_fusion.refs_10_), channel_id=1, source_target_pairs={{128,0},{132,4},{136,8},{140,12},{144,16},{148,20},{152,24},{156,2... | collective-permute-start | bytes 24584 | tf_op jit(solution)/shard_map/ppermute | solution.py:180
  15.4 15.0 %collective-permute-start.18 = (bf16[256,256]{1,0:T(8,128)(2,1)S(1)}, bf16[256,256]{1,0:T(8,128)(2,1)S(1)}, u32[]{:S(2)}, u32[]{:S(2)}) collective-permute-start(bf16[256,256]{1,0:T(8,128)(2,1)S(1)} %constant_dynamic-update-slice_fusion.refs_14_), channel_id=1, source_target_pairs={{40,0},{44,4},{48,8},{52,12},{56,16},{60,20},{0,24},{4,28},{8,32},... | collective-permute-start | bytes 393224 | tf_op jit(solution)/shard_map/ppermute | solution.py:180
  19.4 12.1 %collective-permute-start.16 = (bf16[256,256]{1,0:T(8,128)(2,1)S(1)}, bf16[256,256]{1,0:T(8,128)(2,1)S(1)}, u32[]{:S(2)}, u32[]{:S(2)}) collective-permute-start(bf16[256,256]{1,0:T(8,128)(2,1)S(1)} %constant_dynamic-update-slice_fusion.refs_14_), channel_id=1, source_target_pairs={{32,0},{36,4},{40,8},{44,12},{48,16},{52,20},{56,24},{60,28},{0,32... | collective-permute-start | bytes 393224 | tf_op jit(solution)/shard_map/ppermute | solution.py:180
  20.8 19.9 %collective-permute-start.14 = (bf16[256,256]{1,0:T(8,128)(2,1)S(1)}, bf16[256,256]{1,0:T(8,128)(2,1)S(1)}, u32[]{:S(2)}, u32[]{:S(2)}) collective-permute-start(bf16[256,256]{1,0:T(8,128)(2,1)S(1)} %constant_dynamic-update-slice_fusion.refs_14_), channel_id=1, source_target_pairs={{24,0},{28,4},{32,8},{36,12},{40,16},{44,20},{48,24},{52,28},{56,3... | collective-permute-start | bytes 393224 | tf_op jit(solution)/shard_map/ppermute | solution.py:180
  24.9 17.3 %collective-permute-start.12 = (bf16[256,256]{1,0:T(8,128)(2,1)S(1)}, bf16[256,256]{1,0:T(8,128)(2,1)S(1)}, u32[]{:S(2)}, u32[]{:S(2)}) collective-permute-start(bf16[256,256]{1,0:T(8,128)(2,1)S(1)} %constant_dynamic-update-slice_fusion.refs_14_), channel_id=1, source_target_pairs={{16,0},{20,4},{24,8},{28,12},{32,16},{36,20},{40,24},{44,28},{48,3... | collective-permute-start | bytes 393224 | tf_op jit(solution)/shard_map/ppermute | solution.py:180
  27.6 16.9 %collective-permute-start.10 = (bf16[256,256]{1,0:T(8,128)(2,1)S(1)}, bf16[256,256]{1,0:T(8,128)(2,1)S(1)}, u32[]{:S(2)}, u32[]{:S(2)}) collective-permute-start(bf16[256,256]{1,0:T(8,128)(2,1)S(1)} %constant_dynamic-update-slice_fusion.refs_14_), channel_id=1, source_target_pairs={{8,0},{12,4},{16,8},{20,12},{24,16},{28,20},{32,24},{36,28},{40,32... | collective-permute-start | bytes 393224 | tf_op jit(solution)/shard_map/ppermute | solution.py:180
  30.3 15.0 %collective-permute-start.9 = (bf16[256,256]{1,0:T(8,128)(2,1)S(1)}, bf16[256,256]{1,0:T(8,128)(2,1)S(1)}, u32[]{:S(2)}, u32[]{:S(2)}) collective-permute-start(bf16[256,256]{1,0:T(8,128)(2,1)S(1)} %constant_dynamic-update-slice_fusion.refs_14_), channel_id=1, source_target_pairs={{4,0},{0,4},{12,8},{8,12},{20,16},{16,20},{28,24},{24,28},{36,32},... | collective-permute-start | bytes 393224 | tf_op jit(solution)/shard_map/ppermute | solution.py:180
  31.5 15.0 %collective-permute-start.23 = (bf16[256,256]{1,0:T(8,128)(2,1)S(1)}, bf16[256,256]{1,0:T(8,128)(2,1)S(1)}, u32[]{:S(2)}, u32[]{:S(2)}) collective-permute-start(bf16[256,256]{1,0:T(8,128)(2,1)S(1)} %collective-permute-done.22.refs_28_), channel_id=1, source_target_pairs={{4,0},{0,4},{12,8},{8,12},{20,16},{16,20},{28,24},{24,28},{36,32},... | collective-permute-start | bytes 393224 | tf_op jit(solution)/shard_map/ppermute | solution.py:180
  40.6 6.8 %collective-permute-start.21 = (bf16[256,256]{1,0:T(8,128)(2,1)S(1)}, bf16[256,256]{1,0:T(8,128)(2,1)S(1)}, u32[]{:S(2)}, u32[]{:S(2)}) collective-permute-start(bf16[256,256]{1,0:T(8,128)(2,1)S(1)} %collective-permute-done.20.refs_26_), channel_id=1, source_target_pairs={{4,0},{0,4},{12,8},{8,12},{20,16},{16,20},{28,24},{24,28},{36,32},... | collective-permute-start | bytes 393224 | tf_op jit(solution)/shard_map/ppermute | solution.py:180
  42.2 7.1 %collective-permute-start.19 = (bf16[256,256]{1,0:T(8,128)(2,1)S(1)}, bf16[256,256]{1,0:T(8,128)(2,1)S(1)}, u32[]{:S(2)}, u32[]{:S(2)}) collective-permute-start(bf16[256,256]{1,0:T(8,128)(2,1)S(1)} %collective-permute-done.18.refs_24_), channel_id=1, source_target_pairs={{4,0},{0,4},{12,8},{8,12},{20,16},{16,20},{28,24},{24,28},{36,32},... | collective-permute-start | bytes 393224 | tf_op jit(solution)/shard_map/ppermute | solution.py:180
  44.5 16.1 %collective-permute-start.1 = (bf16[256,512]{1,0:T(8,128)(2,1)S(1)}, bf16[256,512]{1,0:T(8,128)(2,1)S(1)}, u32[]{:S(2)}, u32[]{:S(2)}) collective-permute-start(bf16[256,512]{1,0:T(8,128)(2,1)S(1)} %copy-done.1), channel_id=1, source_target_pairs={{128,0},{132,4},{136,8},{140,12},{144,16},{148,20},{152,24},{156,2... | collective-permute-start | bytes 786440 | tf_op jit(solution)/shard_map/ppermute | solution.py:180
  46.6 8.4 %collective-permute-start.15 = (bf16[256,256]{1,0:T(8,128)(2,1)S(1)}, bf16[256,256]{1,0:T(8,128)(2,1)S(1)}, u32[]{:S(2)}, u32[]{:S(2)}) collective-permute-start(bf16[256,256]{1,0:T(8,128)(2,1)S(1)} %collective-permute-done.14.refs_20_), channel_id=1, source_target_pairs={{4,0},{0,4},{12,8},{8,12},{20,16},{16,20},{28,24},{24,28},{36,32},... | collective-permute-start | bytes 393224 | tf_op jit(solution)/shard_map/ppermute | solution.py:180
  47.4 10.4 %collective-permute-start.13 = (bf16[256,256]{1,0:T(8,128)(2,1)S(1)}, bf16[256,256]{1,0:T(8,128)(2,1)S(1)}, u32[]{:S(2)}, u32[]{:S(2)}) collective-permute-start(bf16[256,256]{1,0:T(8,128)(2,1)S(1)} %collective-permute-done.12.refs_18_), channel_id=1, source_target_pairs={{4,0},{0,4},{12,8},{8,12},{20,16},{16,20},{28,24},{24,28},{36,32},... | collective-permute-start | bytes 393224 | tf_op jit(solution)/shard_map/ppermute | solution.py:180
  49.3 10.3 %collective-permute-start.11 = (bf16[256,256]{1,0:T(8,128)(2,1)S(1)}, bf16[256,256]{1,0:T(8,128)(2,1)S(1)}, u32[]{:S(2)}, u32[]{:S(2)}) collective-permute-start(bf16[256,256]{1,0:T(8,128)(2,1)S(1)} %collective-permute-done.10.refs_16_), channel_id=1, source_target_pairs={{4,0},{0,4},{12,8},{8,12},{20,16},{16,20},{28,24},{24,28},{36,32},... | collective-permute-start | bytes 393224 | tf_op jit(solution)/shard_map/ppermute | solution.py:180
  52.1 10.7 %collective-permute-start = (bf16[256,512]{1,0:T(8,128)(2,1)S(1)}, bf16[256,512]{1,0:T(8,128)(2,1)S(1)}, u32[]{:S(2)}, u32[]{:S(2)}) collective-permute-start(bf16[256,512]{1,0:T(8,128)(2,1)S(1)} %copy-done.1), channel_id=1, source_target_pairs={{64,0},{68,4},{72,8},{76,12},{80,16},{84,20},{88,24},{92,28},{96,3... | collective-permute-start | bytes 786440 | tf_op jit(solution)/shard_map/ppermute | solution.py:180
  55.0 12.9 %collective-permute-start.2 = (bf16[256,512]{1,0:T(8,128)(2,1)S(1)}, bf16[256,512]{1,0:T(8,128)(2,1)S(1)}, u32[]{:S(2)}, u32[]{:S(2)}) collective-permute-start(bf16[256,512]{1,0:T(8,128)(2,1)S(1)} %copy-done.1), channel_id=1, source_target_pairs={{192,0},{196,4},{200,8},{204,12},{208,16},{212,20},{216,24},{220,2... | collective-permute-start | bytes 786440 | tf_op jit(solution)/shard_map/ppermute | solution.py:180
  57.8 16.1 %collective-permute-start.5 = (bf16[256,512]{1,0:T(8,128)(2,1)S(1)}, bf16[256,512]{1,0:T(8,128)(2,1)S(1)}, u32[]{:S(2)}, u32[]{:S(2)}) collective-permute-start(bf16[256,512]{1,0:T(8,128)(2,1)S(1)} %copy-done), channel_id=1, source_target_pairs={{192,0},{196,4},{200,8},{204,12},{208,16},{212,20},{216,24},{220,2... | collective-permute-start | bytes 786440 | tf_op jit(solution)/shard_map/ppermute | solution.py:180
  59.6 14.2 %collective-permute-start.4 = (bf16[256,512]{1,0:T(8,128)(2,1)S(1)}, bf16[256,512]{1,0:T(8,128)(2,1)S(1)}, u32[]{:S(2)}, u32[]{:S(2)}) collective-permute-start(bf16[256,512]{1,0:T(8,128)(2,1)S(1)} %copy-done), channel_id=1, source_target_pairs={{128,0},{132,4},{136,8},{140,12},{144,16},{148,20},{152,24},{156,2... | collective-permute-start | bytes 786440 | tf_op jit(solution)/shard_map/ppermute | solution.py:180
  60.6 13.3 %collective-permute-start.3 = (bf16[256,512]{1,0:T(8,128)(2,1)S(1)}, bf16[256,512]{1,0:T(8,128)(2,1)S(1)}, u32[]{:S(2)}, u32[]{:S(2)}) collective-permute-start(bf16[256,512]{1,0:T(8,128)(2,1)S(1)} %copy-done), channel_id=1, source_target_pairs={{64,0},{68,4},{72,8},{76,12},{80,16},{84,20},{88,24},{92,28},{96,3... | collective-permute-start | bytes 786440 | tf_op jit(solution)/shard_map/ppermute | solution.py:180
  106.3 21.1 %collective-permute-start.27 = (bf16[8,256,256]{2,1,0:T(8,128)(2,1)S(1)}, bf16[8,256,256]{2,1,0:T(8,128)(2,1)S(1)}, u32[]{:S(2)}, u32[]{:S(2)}) collective-permute-start(bf16[8,256,256]{2,1,0:T(8,128)(2,1)S(1)} %get-tuple-element.10), channel_id=1, source_target_pairs={{4,0},{0,4},{12,8},{8,12},{20,16},{16,20},{28,24},{24,28},{36,32},... | collective-permute-start | bytes 3145736 | tf_op jit(solution)/shard_map/ppermute | solution.py:180
  107.6 25.1 %collective-permute-start.24 = (bf16[256,512]{1,0:T(8,128)(2,1)S(1)}, bf16[256,512]{1,0:T(8,128)(2,1)S(1)}, u32[]{:S(2)}, u32[]{:S(2)}) collective-permute-start(bf16[256,512]{1,0:T(8,128)(2,1)S(1)} %get-tuple-element.20), channel_id=1, source_target_pairs={{192,0},{196,4},{200,8},{204,12},{208,16},{212,20},{216,24},{220,2... | collective-permute-start | bytes 786440 | tf_op jit(solution)/shard_map/ppermute | solution.py:180
  107.9 26.1 %collective-permute-start.26 = (bf16[256,512]{1,0:T(8,128)(2,1)S(1)}, bf16[256,512]{1,0:T(8,128)(2,1)S(1)}, u32[]{:S(2)}, u32[]{:S(2)}) collective-permute-start(bf16[256,512]{1,0:T(8,128)(2,1)S(1)} %get-tuple-element.21), channel_id=1, source_target_pairs={{64,0},{68,4},{72,8},{76,12},{80,16},{84,20},{88,24},{92,28},{96,3... | collective-permute-start | bytes 786440 | tf_op jit(solution)/shard_map/ppermute | solution.py:180
  110.9 24.4 %collective-permute-start.25 = (bf16[256,512]{1,0:T(8,128)(2,1)S(1)}, bf16[256,512]{1,0:T(8,128)(2,1)S(1)}, u32[]{:S(2)}, u32[]{:S(2)}) collective-permute-start(bf16[256,512]{1,0:T(8,128)(2,1)S(1)} %get-tuple-element.22), channel_id=1, source_target_pairs={{128,0},{132,4},{136,8},{140,12},{144,16},{148,20},{152,24},{156,2... | collective-permute-start | bytes 786440 | tf_op jit(solution)/shard_map/ppermute | solution.py:180
  127.8 12.8 %collective-permute-start.28 = (bf16[256,256]{1,0:T(8,128)(2,1)S(1)}, bf16[256,256]{1,0:T(8,128)(2,1)S(1)}, u32[]{:S(2)}, u32[]{:S(2)}) collective-permute-start(bf16[256,256]{1,0:T(8,128)(2,1)S(1)} %get-tuple-element.13), channel_id=1, source_target_pairs={{56,0},{60,4},{0,8},{4,12},{8,16},{12,20},{16,24},{20,28},{24,32},... | collective-permute-start | bytes 393224 | tf_op jit(solution)/shard_map/ppermute | solution.py:180
  132.1 9.0 %collective-permute-start.34 = (bf16[256,256]{1,0:T(8,128)(2,1)S(1)}, bf16[256,256]{1,0:T(8,128)(2,1)S(1)}, u32[]{:S(2)}, u32[]{:S(2)}) collective-permute-start(bf16[256,256]{1,0:T(8,128)(2,1)S(1)} %get-tuple-element.14), channel_id=1, source_target_pairs={{8,0},{12,4},{16,8},{20,12},{24,16},{28,20},{32,24},{36,28},{40,32... | collective-permute-start | bytes 393224 | tf_op jit(solution)/shard_map/ppermute | solution.py:180
  132.7 10.8 %collective-permute-start.33 = (bf16[256,256]{1,0:T(8,128)(2,1)S(1)}, bf16[256,256]{1,0:T(8,128)(2,1)S(1)}, u32[]{:S(2)}, u32[]{:S(2)}) collective-permute-start(bf16[256,256]{1,0:T(8,128)(2,1)S(1)} %get-tuple-element.15), channel_id=1, source_target_pairs={{16,0},{20,4},{24,8},{28,12},{32,16},{36,20},{40,24},{44,28},{48,3... | collective-permute-start | bytes 393224 | tf_op jit(solution)/shard_map/ppermute | solution.py:180
  134.1 19.2 %collective-permute-start.32 = (bf16[256,256]{1,0:T(8,128)(2,1)S(1)}, bf16[256,256]{1,0:T(8,128)(2,1)S(1)}, u32[]{:S(2)}, u32[]{:S(2)}) collective-permute-start(bf16[256,256]{1,0:T(8,128)(2,1)S(1)} %get-tuple-element.16), channel_id=1, source_target_pairs={{24,0},{28,4},{32,8},{36,12},{40,16},{44,20},{48,24},{52,28},{56,3... | collective-permute-start | bytes 393224 | tf_op jit(solution)/shard_map/ppermute | solution.py:180
  135.3 18.0 %collective-permute-start.31 = (bf16[256,256]{1,0:T(8,128)(2,1)S(1)}, bf16[256,256]{1,0:T(8,128)(2,1)S(1)}, u32[]{:S(2)}, u32[]{:S(2)}) collective-permute-start(bf16[256,256]{1,0:T(8,128)(2,1)S(1)} %get-tuple-element.17), channel_id=1, source_target_pairs={{32,0},{36,4},{40,8},{44,12},{48,16},{52,20},{56,24},{60,28},{0,32... | collective-permute-start | bytes 393224 | tf_op jit(solution)/shard_map/ppermute | solution.py:180
  140.6 16.9 %collective-permute-start.30 = (bf16[256,256]{1,0:T(8,128)(2,1)S(1)}, bf16[256,256]{1,0:T(8,128)(2,1)S(1)}, u32[]{:S(2)}, u32[]{:S(2)}) collective-permute-start(bf16[256,256]{1,0:T(8,128)(2,1)S(1)} %get-tuple-element.18), channel_id=1, source_target_pairs={{40,0},{44,4},{48,8},{52,12},{56,16},{60,20},{0,24},{4,28},{8,32},... | collective-permute-start | bytes 393224 | tf_op jit(solution)/shard_map/ppermute | solution.py:180
  141.1 16.4 %collective-permute-start.29 = (bf16[256,256]{1,0:T(8,128)(2,1)S(1)}, bf16[256,256]{1,0:T(8,128)(2,1)S(1)}, u32[]{:S(2)}, u32[]{:S(2)}) collective-permute-start(bf16[256,256]{1,0:T(8,128)(2,1)S(1)} %get-tuple-element.19), channel_id=1, source_target_pairs={{48,0},{52,4},{56,8},{60,12},{0,16},{4,20},{8,24},{12,28},{16,32},... | collective-permute-start | bytes 393224 | tf_op jit(solution)/shard_map/ppermute | solution.py:180
  (7 other events, 191.0 us)

commit v2 on v1

v2 whole, which is shorter than its diff:
```python
import math

import jax
import jax.numpy as jnp
from jax import lax
from jax.experimental import pallas as pl
from jax.experimental.pallas import tpu as pltpu
from jax.sharding import PartitionSpec as P

F32 = jnp.float32
BF16 = jnp.bfloat16
HEAD = 128
HEADS = 4
HALF = 128
ROWS = HEADS * HALF
NY, NZ, NX = 4, 8, 2
SCALE = 1.0 / math.sqrt(HEAD)
LOG2E = math.log2(math.e)
NT = (((1,), (1,)), ((), ()))
TN = (((0,), (0,)), ((), ()))
PACK = 2 * 2 * ROWS
STATS = 48
OPEN = (0, 1, 2, 3, 6, 7)
STAGES = ((4, 5), (3, 6), (2, 7), (1, 0))


def dot(a, b, dims):
    return lax.dot_general(a, b, dims, preferred_element_type=F32)


def pack_kernel(q_in, g_in, o_in, n_in, k_in, v_in, pack, kv, q_ref, g_ref, o_ref, n_ref, k_ref, v_ref, sems):
    pairs = [(k_in, k_ref), (v_in, v_ref), (q_in, q_ref), (g_in, g_ref), (o_in, o_ref), (n_in, n_ref)]
    copies = [pltpu.make_async_copy(s, t, sems.at[i]) for i, (s, t) in enumerate(pairs)]
    for copy in copies:
        copy.start()
    for copy in copies:
        copy.wait()
    for half in range(2):
        rows = slice(half * HALF, (half + 1) * HALF)
        kv[half, 0] = k_ref[rows, :]
        kv[half, 1] = v_ref[rows, :]
    terms = []
    for half in range(2):
        rows = slice(half * HALF, (half + 1) * HALF)
        deltas = []
        for h in range(HEADS):
            cols = slice(h * HEAD, (h + 1) * HEAD)
            q, g = q_ref[rows, cols], g_ref[rows, cols]
            at = half * 2 * ROWS + h * HALF
            pack[at : at + HALF, :] = q
            pack[at + ROWS : at + ROWS + HALF, :] = g
            product = o_ref[rows, cols].astype(F32) * g.astype(F32)
            deltas.append(jnp.sum(product.T, axis=0, keepdims=True))
        rest = jnp.concatenate([n_ref[:, rows] * LOG2E] + deltas, axis=0)
        for _ in range(3):
            term = rest.astype(BF16).astype(F32)
            rest = rest - term
            terms.append(term)
    pack[PACK:, :] = jnp.concatenate(terms, axis=0).astype(BF16)


def pack_inputs(queries, out_grads, attn_out, log_norms, key_head, value_head):
    vmem = pl.BlockSpec(memory_space=pltpu.VMEM)
    arrays = (queries, out_grads, attn_out, log_norms, key_head, value_head)
    return pl.pallas_call(
        pack_kernel,
        out_shape=(
            jax.ShapeDtypeStruct((PACK + STATS, HEAD), BF16),
            jax.ShapeDtypeStruct((2, 2, HALF, HEAD), BF16),
        ),
        in_specs=[pl.BlockSpec(memory_space=pl.ANY)] * 6,
        out_specs=(vmem,) * 2,
        scratch_shapes=[pltpu.VMEM(array.shape, array.dtype) for array in arrays]
        + [pltpu.SemaphoreType.DMA((6,))],
        compiler_params=pltpu.CompilerParams(vmem_limit_bytes=56 * 1024 * 1024),
    )(*arrays)


def stage_kernel(near, is_first, is_last, *refs):
    m = len(near)
    n_k = NX * m
    me_ref, pairing = refs[:2]
    packs = refs[2 : 2 + NY]
    blocks = refs[2 + NY : 2 + NY + m]
    at = 2 + NY + m
    acc_in = None
    if not is_first:
        acc_in = refs[at]
        at += 1
    dkv_refs = refs[at : at + m]
    at += m
    if is_last:
        dq_refs = refs[at : at + NY]
        at += NY
        acc = refs[at]
    else:
        acc = refs[at]
    at += 1
    ns, ds, ks, vs, dks, dvs, rk = refs[at:]

    me = me_ref[0]
    x, z, y = me & 1, (me >> 1) & (NZ - 1), me >> 4
    rq = [pairing[index_of((y + d) & (NY - 1), z, x)] for d in range(NY)]
    for i, r in enumerate(near):
        for s in range(NX):
            rk[NX * i + s] = pairing[index_of(y, (z + r) & (NZ - 1), x ^ s)]
            e = NX * i + s
            for half in range(2):
                ks[half, e * HALF : (e + 1) * HALF, :] = blocks[i][s, half, 0]
                vs[half, e * HALF : (e + 1) * HALF, :] = blocks[i][s, half, 1]
    for d in range(NY):
        terms = packs[d][PACK:, :].astype(F32)
        for half in range(2):
            t = terms[24 * half : 24 * half + 24]
            stat = (t[0:8] + t[8:16]) + t[16:24]
            for h in range(HEADS):
                cols = slice(h * HALF, (h + 1) * HALF)
                ns[2 * d + half, :, cols] = stat[h : h + 1]
                ds[2 * d + half, :, cols] = stat[HEADS + h : HEADS + h + 1]
    acc[...] = jnp.zeros_like(acc) if is_first else acc_in[...]

    def tile(d, half, k, v, keep=None):
        i = 2 * d + half
        q = packs[d][pl.ds(pl.multiple_of(half * (2 * ROWS), ROWS), ROWS), :]
        g = packs[d][pl.ds(pl.multiple_of(half * (2 * ROWS) + ROWS, ROWS), ROWS), :]
        scores = dot(k, q, NT)
        probs = jnp.exp2(scores * (SCALE * LOG2E) - ns[i])
        if keep is not None:
            probs = jnp.where(keep, probs, 0.0)
        dprobs = dot(v, g, NT)
        dscores = (probs * (dprobs - ds[i]) * SCALE).astype(BF16)
        probs_low = probs.astype(BF16)
        dv = jnp.dot(probs_low, g, preferred_element_type=F32)
        dk = jnp.dot(dscores, q, preferred_element_type=F32)
        acc[i] += dot(k, dscores, TN)
        return dk, dv

    chunk = 4 if n_k % 4 == 0 else 3

    def first(c, carry):
        keys = pl.ds(pl.multiple_of(c * (chunk * HALF), chunk * HALF), chunk * HALF)
        k, v = ks[0, keys, :], vs[0, keys, :]
        dk = dv = 0.0
        for d in range(NY):
            dk_part, dv_part = tile(d, 1, k, v)
            dk, dv = dk + dk_part, dv + dv_part
        dks[0, keys, :] = dk
        dvs[0, keys, :] = dv
        dks[1, keys, :] = jnp.zeros_like(dk)
        dvs[1, keys, :] = jnp.zeros_like(dv)
        return carry

    lax.fori_loop(0, n_k // chunk, first, 0)

    def second(e, d):
        half = jnp.where(rk[e] < rq[d], 0, 1)
        keys = pl.ds(pl.multiple_of(e * HALF, HALF), HALF)
        dk, dv = tile(d, half, ks[half, keys, :], vs[half, keys, :])
        dks[half, keys, :] += dk
        dvs[half, keys, :] += dv

    def second_all(e, carry):
        for d in range(NY):
            second(e, d)
        return carry

    has_own = near[-1] == 0
    own_e = n_k - NX
    lax.fori_loop(0, own_e if has_own else n_k, second_all, 0)
    if has_own:
        second_all(own_e + 1, 0)
        for d in range(1, NY):
            second(own_e, d)
        keys = slice(own_e * HALF, (own_e + 1) * HALF)
        key_at = lax.broadcasted_iota(jnp.int32, (HALF, ROWS), 0)
        row_at = lax.broadcasted_iota(jnp.int32, (HALF, ROWS), 1) & (HALF - 1)
        keep = row_at >= key_at
        for half in range(2):
            dk, dv = tile(0, half, ks[half, keys, :], vs[half, keys, :], keep)
            dks[half, keys, :] += dk
            dvs[half, keys, :] += dv
    if is_last:
        for d in range(NY):
            for half in range(2):
                rows = slice(half * HALF, (half + 1) * HALF)
                for h in range(HEADS):
                    cols = slice(h * HEAD, (h + 1) * HEAD)
                    block = acc[2 * d + half, :, cols].T
                    dq_refs[d][rows, cols] = block if d == 0 else block.astype(BF16)
    for i, r in enumerate(near):
        for s in range(NX):
            for half in range(2):
                rows = slice(half * HALF, (half + 1) * HALF)
                e = NX * i + s
                keys = slice(e * HALF, (e + 1) * HALF)
                dk, dv = dks[half, keys, :], dvs[half, keys, :]
                out = dkv_refs[i].at[s]
                out[rows, :HEAD] = dk.astype(out.dtype)
                out[rows, HEAD:] = dv.astype(out.dtype)


def stage(near, me, pairing, packs, blocks, acc, is_last):
    m = len(near)
    pairs = NY * NX * m
    smem = pl.BlockSpec(memory_space=pltpu.SMEM)
    vmem = pl.BlockSpec(memory_space=pltpu.VMEM)
    sums = jax.ShapeDtypeStruct((2 * NY, HEAD, ROWS), F32)
    outs = [jax.ShapeDtypeStruct((NX, 2 * HALF, 2 * HEAD), F32 if r in OPEN else BF16) for r in near]
    if is_last:
        outs += [jax.ShapeDtypeStruct((2 * HALF, ROWS), F32 if d == 0 else BF16) for d in range(NY)]
    else:
        outs += [sums]
    first = [] if acc is None else [acc]

    def kernel(*refs):
        stage_kernel(near, acc is None, is_last, *refs)

    scratch = [pltpu.VMEM(sums.shape, F32)] if is_last else []
    return pl.pallas_call(
        kernel,
        out_shape=tuple(outs),
        in_specs=[smem, smem] + [vmem] * (NY + m + len(first)),
        out_specs=(vmem,) * len(outs),
        scratch_shapes=scratch
        + [
            pltpu.VMEM((2 * NY, 1, ROWS), F32),
            pltpu.VMEM((2 * NY, 1, ROWS), F32),
            pltpu.VMEM((2, NX * m * HALF, HEAD), BF16),
            pltpu.VMEM((2, NX * m * HALF, HEAD), BF16),
            pltpu.VMEM((2, NX * m * HALF, HEAD), F32),
            pltpu.VMEM((2, NX * m * HALF, HEAD), F32),
            pltpu.SMEM((NX * m,), jnp.int32),
        ],
        compiler_params=pltpu.CompilerParams(vmem_limit_bytes=32 * 1024 * 1024),
        cost_estimate=pl.CostEstimate(
            flops=pairs * 2 * 5 * 2 * HALF * HALF * ROWS * 2,
            bytes_accessed=4 * 1024 * 1024,
            transcendentals=pairs * 2 * HALF * ROWS,
        ),
    )(me, pairing, *packs, *blocks, *first)


def index_of(y, z, x):
    return (y * NZ + z) * NX + x


def shift(dy, dz, flip):
    return [
        (index_of((y + dy) % NY, (z + dz) % NZ, x ^ flip), index_of(y, z, x))
        for y in range(NY)
        for z in range(NZ)
        for x in range(NX)
    ]


def fetch(array, dy=0, dz=0, flip=0):
    return lax.ppermute(array, "ctx", shift(dy % NY, dz % NZ, flip))


def body(queries, key_head, value_head, attn_out, out_grads, log_norms, pairing):
    me = jnp.full((1,), lax.axis_index("ctx"), jnp.int32)
    pack, kv = pack_inputs(queries, out_grads, attn_out, log_norms, key_head, value_head)
    packs = {0: pack, 1: fetch(pack, dy=1), 3: fetch(pack, dy=-1)}
    packs[2] = fetch(packs[1], dy=1)
    blocks = {0: jnp.stack([kv, fetch(kv, flip=1)])}
    for r in (1, 2, 3):
        blocks[r] = fetch(blocks[r - 1], dz=1)
        blocks[NZ - r] = fetch(blocks[(NZ - r + 1) % NZ], dz=-1)
    blocks[4] = fetch(blocks[3], dz=1)

    acc = None
    up = down = None
    for at, near in enumerate(STAGES):
        is_last = at == len(STAGES) - 1
        outs = stage(near, me, pairing, [packs[d] for d in range(NY)], [blocks[r] for r in near], acc, is_last)
        acc = outs[2]
        if at == 0:
            up, down = outs[0], outs[1]
        elif not is_last:
            up = (outs[0] + up.astype(F32)).astype(BF16)
            down = (outs[1] + down.astype(F32)).astype(BF16)
        else:
            up = (outs[0] + up.astype(F32)).astype(BF16)
            dkv = outs[1] + down.astype(F32)
        up = fetch(up, dz=-1)
        if not is_last:
            down = fetch(down, dz=1)
    dq = acc
    for d in range(1, NY):
        dq = dq + fetch(outs[2 + d], dy=-d).astype(F32)
    dkv = dkv + up.astype(F32)
    dkv = dkv[0] + fetch(dkv[1].astype(BF16), flip=1).astype(F32)
    return dq, dkv[:, :HEAD], dkv[:, HEAD:]


def solution(mesh):
    rows = P(("dp", "ctx"), None)
    in_specs = (rows,) * 5 + (P(None, ("dp", "ctx")), P("dp"))
    return jax.shard_map(
        body, mesh=mesh, in_specs=in_specs, out_specs=(rows,) * 3, check_vma=False
    )
```

time: 161 us -> 104 us (0.65); the launches traced: 158 us -> 104 us
  waiting for transfers between devices: 60.2 us -> 18.6 us
  starting transfers between devices: 58.9 us -> 43.3 us
  Pallas kernels: 32.4 us -> 36.3 us
    ppermute x35 -> x22, waiting for transfers between devices: 60.2 us -> 18.6 us  [fetch(): return lax.ppermute(array, 'ctx', shift(dy % NY, dz % NZ, flip))]
    ppermute x35 -> x22, starting transfers between devices: 58.9 us -> 43.3 us  [fetch(): return lax.ppermute(array, 'ctx', shift(dy % NY, dz % NZ, flip))]
    pallas_call x1 -> x5, Pallas kernels: 32.4 us -> 36.3 us  [the longest x4 34 us: stage(): pl.pallas_call(kernel, out_shape=tuple(outs), in_specs=[smem, smem] + [vm...]
  transfers between devices with their start and end apart: 35 -> 22, of which waited for: 15 -> 10; matrix products, arithmetic and copies ran while one was open for 2% -> 2% of each run, Pallas kernels for 0% -> 24%
where the time goes in v2:
time: 104 us
  starting transfers between devices  43.3 us (42%)
  Pallas kernels  36.3 us (35%)
  waiting for transfers between devices  18.6 us (18%)
  local copies, waits for them, and re-layouts  2.43 us (2%)
  other arithmetic  2.26 us (2%)
    ppermute x22, starting transfers between devices, fetch(): return lax.ppermute(array, 'ctx', shift(dy % NY, dz % NZ, flip))  43.3 us
    pallas_call x4, Pallas kernels, stage(): pl.pallas_call(kernel, out_shape=tuple(outs), in_specs=[smem, smem] + [vm...  34 us
    ppermute x22, waiting for transfers between devices, fetch(): return lax.ppermute(array, 'ctx', shift(dy % NY, dz % NZ, flip))  18.6 us
    pallas_call x1, Pallas kernels, pack_inputs(): pl.pallas_call(pack_kernel, out_shape=(jax.ShapeDtypeStruct((PACK + STATS...  2.28 us
  transfers between devices with their start and end apart: 22, of which 10 were waited for; matrix products, arithmetic and copies ran while one was open for 2% of the time, Pallas kernels for 24%

profile of v2, /device:TPU:4, one launch (start us, length us, event | category | flops | bytes accessed | tf_op | source)
XLA Modules:
  0.0 103.6 jit_solution(14937512974643157959)
XLA Ops:
  0.6 2.3 %shard_map.94 = (bf16[2096,128]{1,0:T(8,128)(2,1)}, bf16[2,2,128,128]{3,2,1,0:T(8,128)(2,1)}) custom-call(bf16[256,512]{1,0:T(8,128)(2,1)} %q_in.1, bf16[256,512]{1,0:T(8,128)(2,1)} %g_in.1, bf16[256,512]{1,0:T(8,128)(2,1)} %o_in.1, f32[4,256]{1,0:T(4,128)} %n_in.1, bf16[256,128]{1,0:T(8,128)(2,1)} %k_in.1, bf16[256,128]{1,0:T(8,128)(2,1)} %v_in.1), custom_call_target="tpu_custom_call" | custom-call | tf_op jit(solution)/shard_map/pallas_call | solution.py:65
  2.9 1.3 %collective-permute-start.3 = (bf16[2,2,128,128]{3,2,1,0:T(8,128)(2,1)}, bf16[2,2,128,128]{3,2,1,0:T(8,128)(2,1)S(1)}, u32[]{:S(2)}, u32[]{:S(2)}) collective-permute-start(bf16[2,2,128,128]{3,2,1,0:T(8,128)(2,1)} %get-tuple-element.21), channel_id=1, source_target_pairs={{4,0},{0,4},{12,8},{8,12},{20,16},{16,20},{28,24},{24,28},{36,32},... | collective-permute-start | bytes 393224 | tf_op jit(solution)/shard_map/ppermute | solution.py:257
  4.2 3.0 %collective-permute-start = (bf16[2096,128]{1,0:T(8,128)(2,1)}, bf16[2096,128]{1,0:T(8,128)(2,1)S(1)}, u32[]{:S(2)}, u32[]{:S(2)}) collective-permute-start(bf16[2096,128]{1,0:T(8,128)(2,1)} %get-tuple-element.20.refs_2_), channel_id=1, source_target_pairs={{64,0},{68,4},{72,8},{76,12},{80,16},{84,20},{88,24},{92,28},{96,3... | collective-permute-start | bytes 1609736 | tf_op jit(solution)/shard_map/ppermute | solution.py:257
  7.2 1.2 %collective-permute-done.3 = bf16[2,2,128,128]{3,2,1,0:T(8,128)(2,1)S(1)} collective-permute-done((bf16[2,2,128,128]{3,2,1,0:T(8,128)(2,1)}, bf16[2,2,128,128]{3,2,1,0:T(8,128)(2,1)S(1)}, u32[]{:S(2)}, u32[]{:S(2)}) %collective-permute-start.3) | collective-permute-done | bytes 131104 | tf_op jit(solution)/shard_map/ppermute | solution.py:257
  8.5 0.9 pad_maximum_fusion.refs_7_
  9.4 5.9 %collective-permute-start.4 = (bf16[2,2,2,128,128]{4,3,2,1,0:T(8,128)(2,1)S(1)}, bf16[2,2,2,128,128]{4,3,2,1,0:T(8,128)(2,1)S(1)}, u32[]{:S(2)}, u32[]{:S(2)}) collective-permute-start(bf16[2,2,2,128,128]{4,3,2,1,0:T(8,128)(2,1)S(1)} %pad_maximum_fusion.refs_7_), channel_id=1, source_target_pairs={{8,0},{12,4},{16,8},{20,12},{24,16},{28,20},{32,24},{36,28},{40,32... | collective-permute-start | bytes 786440 | tf_op jit(solution)/shard_map/ppermute | solution.py:257
  15.3 4.7 %collective-permute-done.4.refs_6_ = bf16[2,2,2,128,128]{4,3,2,1,0:T(8,128)(2,1)S(1)} collective-permute-done((bf16[2,2,2,128,128]{4,3,2,1,0:T(8,128)(2,1)S(1)}, bf16[2,2,2,128,128]{4,3,2,1,0:T(8,128)(2,1)S(1)}, u32[]{:S(2)}, u32[]{:S(2)}) %collective-permute-start.4) | collective-permute-done | bytes 262176 | tf_op jit(solution)/shard_map/ppermute | solution.py:257
  20.0 3.7 %collective-permute-start.5 = (bf16[2,2,2,128,128]{4,3,2,1,0:T(8,128)(2,1)S(1)}, bf16[2,2,2,128,128]{4,3,2,1,0:T(8,128)(2,1)S(1)}, u32[]{:S(2)}, u32[]{:S(2)}) collective-permute-start(bf16[2,2,2,128,128]{4,3,2,1,0:T(8,128)(2,1)S(1)} %collective-permute-done.4.refs_6_), channel_id=1, source_target_pairs={{8,0},{12,4},{16,8},{20,12},{24,16},{28,20},{32,24},{36,28},{40,32... | collective-permute-start | bytes 786440 | tf_op jit(solution)/shard_map/ppermute | solution.py:257
  23.7 1.6 %collective-permute-start.2 = (bf16[2096,128]{1,0:T(8,128)(2,1)}, bf16[2096,128]{1,0:T(8,128)(2,1)S(1)}, u32[]{:S(2)}, u32[]{:S(2)}) collective-permute-start(bf16[2096,128]{1,0:T(8,128)(2,1)} %get-tuple-element.20.refs_2_), channel_id=1, source_target_pairs={{192,0},{196,4},{200,8},{204,12},{208,16},{212,20},{216,24},{220,2... | collective-permute-start | bytes 1609736 | tf_op jit(solution)/shard_map/ppermute | solution.py:257
  25.3 1.7 %collective-permute-start.1 = (bf16[2096,128]{1,0:T(8,128)(2,1)S(1)}, bf16[2096,128]{1,0:T(8,128)(2,1)S(1)}, u32[]{:S(2)}, u32[]{:S(2)}) collective-permute-start(bf16[2096,128]{1,0:T(8,128)(2,1)S(1)} %collective-permute-done.refs_3_), channel_id=1, source_target_pairs={{64,0},{68,4},{72,8},{76,12},{80,16},{84,20},{88,24},{92,28},{96,3... | collective-permute-start | bytes 1609736 | tf_op jit(solution)/shard_map/ppermute | solution.py:257
  27.6 3.7 %collective-permute-start.7 = (bf16[2,2,2,128,128]{4,3,2,1,0:T(8,128)(2,1)S(1)}, bf16[2,2,2,128,128]{4,3,2,1,0:T(8,128)(2,1)S(1)}, u32[]{:S(2)}, u32[]{:S(2)}) collective-permute-start(bf16[2,2,2,128,128]{4,3,2,1,0:T(8,128)(2,1)S(1)} %collective-permute-done.5.refs_6_), channel_id=1, source_target_pairs={{8,0},{12,4},{16,8},{20,12},{24,16},{28,20},{32,24},{36,28},{40,32... | collective-permute-start | bytes 786440 | tf_op jit(solution)/shard_map/ppermute | solution.py:257
  31.3 3.2 %collective-permute-done.8.refs_7_ = bf16[2,2,2,128,128]{4,3,2,1,0:T(8,128)(2,1)S(1)} collective-permute-done((bf16[2,2,2,128,128]{4,3,2,1,0:T(8,128)(2,1)S(1)}, bf16[2,2,2,128,128]{4,3,2,1,0:T(8,128)(2,1)S(1)}, u32[]{:S(2)}, u32[]{:S(2)}) %collective-permute-start.8) | collective-permute-done | bytes 262176 | tf_op jit(solution)/shard_map/ppermute | solution.py:257
  34.5 0.7 collective-permute-done.7.refs_6_
  35.3 3.7 %collective-permute-start.9 = (bf16[2,2,2,128,128]{4,3,2,1,0:T(8,128)(2,1)S(1)}, bf16[2,2,2,128,128]{4,3,2,1,0:T(8,128)(2,1)}, u32[]{:S(2)}, u32[]{:S(2)}) collective-permute-start(bf16[2,2,2,128,128]{4,3,2,1,0:T(8,128)(2,1)S(1)} %collective-permute-done.7.refs_6_), channel_id=1, source_target_pairs={{8,0},{12,4},{16,8},{20,12},{24,16},{28,20},{32,24},{36,28},{40,32... | collective-permute-start | bytes 786440 | tf_op jit(solution)/shard_map/ppermute | solution.py:257
  39.0 3.2 %collective-permute-done.10.refs_7_ = bf16[2,2,2,128,128]{4,3,2,1,0:T(8,128)(2,1)S(1)} collective-permute-done((bf16[2,2,2,128,128]{4,3,2,1,0:T(8,128)(2,1)S(1)}, bf16[2,2,2,128,128]{4,3,2,1,0:T(8,128)(2,1)S(1)}, u32[]{:S(2)}, u32[]{:S(2)}) %collective-permute-start.10) | collective-permute-done | bytes 262176 | tf_op jit(solution)/shard_map/ppermute | solution.py:257
  42.1 0.7 collective-permute-done.9.refs_6_
  42.9 1.0 %copy-done = bf16[2096,128]{1,0:T(8,128)(2,1)S(1)} copy-done((bf16[2096,128]{1,0:T(8,128)(2,1)S(1)}, bf16[2096,128]{1,0:T(8,128)(2,1)}, u32[]{:S(2)}) %copy-start) | copy-done | bytes 536600
  44.6 8.7 %shard_map.95 = (bf16[2,256,256]{2,1,0:T(8,128)(2,1)S(1)}, bf16[2,256,256]{2,1,0:T(8,128)(2,1)S(1)}, f32[8,128,512]{2,1,0:T(8,128)S(1)}) custom-call(s32[1]{0:T(128)} %bitcast.refs_0_, s32[64]{0:T(128)S(1)} %copy-done.1, bf16[2096,128]{1,0:T(8,128)(2,1)S(1)} %copy-done, bf16[2096,128]{1,0:T(8,128)(2,1)S(1)} %collective-permute-done.refs_3_, ...), custom_call_target="tpu_custom_call" | custom-call | flops 5368709120 | bytes 4194304 | tf_op jit(solution)/shard_map/pallas_call | solution.py:219
  53.3 4.1 %collective-permute-start.14 = (bf16[2,256,256]{2,1,0:T(8,128)(2,1)S(1)}, bf16[2,256,256]{2,1,0:T(8,128)(2,1)S(1)}, u32[]{:S(2)}, u32[]{:S(2)}) collective-permute-start(bf16[2,256,256]{2,1,0:T(8,128)(2,1)S(1)} %get-tuple-element.32), channel_id=1, source_target_pairs={{8,0},{12,4},{16,8},{20,12},{24,16},{28,20},{32,24},{36,28},{40,32... | collective-permute-start | bytes 786440 | tf_op jit(solution)/shard_map/ppermute | solution.py:257
  57.4 8.3 %shard_map.96 = (f32[2,256,256]{2,1,0:T(8,128)S(1)}, f32[2,256,256]{2,1,0:T(8,128)S(1)}, f32[8,128,512]{2,1,0:T(8,128)S(1)}) custom-call(s32[1]{0:T(128)} %bitcast.refs_0_, s32[64]{0:T(128)S(1)} %copy-done.1, bf16[2096,128]{1,0:T(8,128)(2,1)S(1)} %copy-done, bf16[2096,128]{1,0:T(8,128)(2,1)S(1)} %collective-permute-done.refs_3_, ...), custom_call_target="tpu_custom_call" | custom-call | flops 5368709120 | bytes 4194304 | tf_op jit(solution)/shard_map/pallas_call | solution.py:219
  65.8 8.3 %shard_map.97 = (f32[2,256,256]{2,1,0:T(8,128)S(1)}, f32[2,256,256]{2,1,0:T(8,128)S(1)}, f32[8,128,512]{2,1,0:T(8,128)S(1)}) custom-call(s32[1]{0:T(128)} %bitcast.refs_0_, s32[64]{0:T(128)S(1)} %copy-done.1, bf16[2096,128]{1,0:T(8,128)(2,1)S(1)} %copy-done, bf16[2096,128]{1,0:T(8,128)(2,1)S(1)} %collective-permute-done.refs_3_, ...), custom_call_target="tpu_custom_call" | custom-call | flops 5368709120 | bytes 4194304 | tf_op jit(solution)/shard_map/pallas_call | solution.py:219
  74.2 3.3 %collective-permute-start.15 = (bf16[2,256,256]{2,1,0:T(8,128)(2,1)S(1)}, bf16[2,256,256]{2,1,0:T(8,128)(2,1)S(1)}, u32[]{:S(2)}, u32[]{:S(2)}) collective-permute-start(bf16[2,256,256]{2,1,0:T(8,128)(2,1)S(1)} %add_convert_fusion.4), channel_id=1, source_target_pairs={{8,0},{12,4},{16,8},{20,12},{24,16},{28,20},{32,24},{36,28},{40,32... | collective-permute-start | bytes 786440 | tf_op jit(solution)/shard_map/ppermute | solution.py:257
  77.9 8.7 %shard_map.98 = (f32[2,256,256]{2,1,0:T(8,128)S(1)}, f32[2,256,256]{2,1,0:T(8,128)S(1)}, f32[256,512]{1,0:T(8,128)S(1)}, bf16[256,512]{1,0:T(8,128)(2,1)S(1)}, b...) custom-call(s32[1]{0:T(128)} %bitcast.refs_0_, s32[64]{0:T(128)S(1)} %copy-done.1, ...), custom_call_target="tpu_custom_call" | custom-call | flops 5368709120 | bytes 4194304 | tf_op jit(solution)/shard_map/pallas_call | solution.py:219
  86.7 3.3 %collective-permute-start.16 = (bf16[2,256,256]{2,1,0:T(8,128)(2,1)S(1)}, bf16[2,256,256]{2,1,0:T(8,128)(2,1)S(1)}, u32[]{:S(2)}, u32[]{:S(2)}) collective-permute-start(bf16[2,256,256]{2,1,0:T(8,128)(2,1)S(1)} %add_convert_fusion.3), channel_id=1, source_target_pairs={{8,0},{12,4},{16,8},{20,12},{24,16},{28,20},{32,24},{36,28},{40,32... | collective-permute-start | bytes 786440 | tf_op jit(solution)/shard_map/ppermute | solution.py:257
  90.1 2.1 %collective-permute-start.11 = (bf16[256,512]{1,0:T(8,128)(2,1)S(1)}, bf16[256,512]{1,0:T(8,128)(2,1)S(1)}, u32[]{:S(2)}, u32[]{:S(2)}) collective-permute-start(bf16[256,512]{1,0:T(8,128)(2,1)S(1)} %get-tuple-element.26), channel_id=1, source_target_pairs={{192,0},{196,4},{200,8},{204,12},{208,16},{212,20},{216,24},{220,2... | collective-permute-start | bytes 786440 | tf_op jit(solution)/shard_map/ppermute | solution.py:257
  92.2 2.5 %collective-permute-start.12 = (bf16[256,512]{1,0:T(8,128)(2,1)S(1)}, bf16[256,512]{1,0:T(8,128)(2,1)S(1)}, u32[]{:S(2)}, u32[]{:S(2)}) collective-permute-start(bf16[256,512]{1,0:T(8,128)(2,1)S(1)} %get-tuple-element.27), channel_id=1, source_target_pairs={{128,0},{132,4},{136,8},{140,12},{144,16},{148,20},{152,24},{156,2... | collective-permute-start | bytes 786440 | tf_op jit(solution)/shard_map/ppermute | solution.py:257
  94.7 1.8 %collective-permute-start.13 = (bf16[256,512]{1,0:T(8,128)(2,1)S(1)}, bf16[256,512]{1,0:T(8,128)(2,1)S(1)}, u32[]{:S(2)}, u32[]{:S(2)}) collective-permute-start(bf16[256,512]{1,0:T(8,128)(2,1)S(1)} %get-tuple-element.28), channel_id=1, source_target_pairs={{64,0},{68,4},{72,8},{76,12},{80,16},{84,20},{88,24},{92,28},{96,3... | collective-permute-start | bytes 786440 | tf_op jit(solution)/shard_map/ppermute | solution.py:257
  96.4 1.3 %collective-permute-done.20 = bf16[2,256,256]{2,1,0:T(8,128)(2,1)S(1)} collective-permute-done((bf16[2,256,256]{2,1,0:T(8,128)(2,1)S(1)}, bf16[2,256,256]{2,1,0:T(8,128)(2,1)S(1)}, u32[]{:S(2)}, u32[]{:S(2)}) %collective-permute-start.20) | collective-permute-done | bytes 262176 | tf_op jit(solution)/shard_map/ppermute | solution.py:257
  97.8 1.3 %collective-permute-start.21 = (bf16[256,256]{1,0:T(8,128)(2,1)S(1)}, bf16[256,256]{1,0:T(8,128)(2,1)S(1)}, u32[]{:S(2)}, u32[]{:S(2)}) collective-permute-start(bf16[256,256]{1,0:T(8,128)(2,1)S(1)} %fusion.1), channel_id=1, source_target_pairs={{4,0},{0,4},{12,8},{8,12},{20,16},{16,20},{28,24},{24,28},{36,32},... | collective-permute-start | bytes 393224 | tf_op jit(solution)/shard_map/ppermute | solution.py:257
  99.1 2.7 %collective-permute-done.12 = bf16[256,512]{1,0:T(8,128)(2,1)S(1)} collective-permute-done((bf16[256,512]{1,0:T(8,128)(2,1)S(1)}, bf16[256,512]{1,0:T(8,128)(2,1)S(1)}, u32[]{:S(2)}, u32[]{:S(2)}) %collective-permute-start.12) | collective-permute-done | bytes 262176 | tf_op jit(solution)/shard_map/ppermute | solution.py:257
  101.8 0.9 convert_add_fusion.1
  102.9 0.7 fusion.2
  (32 shorter events, 2.3 us)
Async XLA Ops:
  2.9 5.5 %collective-permute-start.3 = (bf16[2,2,128,128]{3,2,1,0:T(8,128)(2,1)}, bf16[2,2,128,128]{3,2,1,0:T(8,128)(2,1)S(1)}, u32[]{:S(2)}, u32[]{:S(2)}) collective-permute-start(bf16[2,2,128,128]{3,2,1,0:T(8,128)(2,1)} %get-tuple-element.21), channel_id=1, source_target_pairs={{4,0},{0,4},{12,8},{8,12},{20,16},{16,20},{28,24},{24,28},{36,32},... | collective-permute-start | bytes 393224 | tf_op jit(solution)/shard_map/ppermute | solution.py:257
  4.2 21.1 %collective-permute-start = (bf16[2096,128]{1,0:T(8,128)(2,1)}, bf16[2096,128]{1,0:T(8,128)(2,1)S(1)}, u32[]{:S(2)}, u32[]{:S(2)}) collective-permute-start(bf16[2096,128]{1,0:T(8,128)(2,1)} %get-tuple-element.20.refs_2_), channel_id=1, source_target_pairs={{64,0},{68,4},{72,8},{76,12},{80,16},{84,20},{88,24},{92,28},{96,3... | collective-permute-start | bytes 1609736 | tf_op jit(solution)/shard_map/ppermute | solution.py:257
  9.4 10.6 %collective-permute-start.4 = (bf16[2,2,2,128,128]{4,3,2,1,0:T(8,128)(2,1)S(1)}, bf16[2,2,2,128,128]{4,3,2,1,0:T(8,128)(2,1)S(1)}, u32[]{:S(2)}, u32[]{:S(2)}) collective-permute-start(bf16[2,2,2,128,128]{4,3,2,1,0:T(8,128)(2,1)S(1)} %pad_maximum_fusion.refs_7_), channel_id=1, source_target_pairs={{8,0},{12,4},{16,8},{20,12},{24,16},{28,20},{32,24},{36,28},{40,32... | collective-permute-start | bytes 786440 | tf_op jit(solution)/shard_map/ppermute | solution.py:257
  15.3 11.6 %collective-permute-start.6 = (bf16[2,2,2,128,128]{4,3,2,1,0:T(8,128)(2,1)S(1)}, bf16[2,2,2,128,128]{4,3,2,1,0:T(8,128)(2,1)S(1)}, u32[]{:S(2)}, u32[]{:S(2)}) collective-permute-start(bf16[2,2,2,128,128]{4,3,2,1,0:T(8,128)(2,1)S(1)} %pad_maximum_fusion.refs_7_), channel_id=1, source_target_pairs={{56,0},{60,4},{0,8},{4,12},{8,16},{12,20},{16,24},{20,28},{24,32},... | collective-permute-start | bytes 786440 | tf_op jit(solution)/shard_map/ppermute | solution.py:257
  20.0 7.6 %collective-permute-start.5 = (bf16[2,2,2,128,128]{4,3,2,1,0:T(8,128)(2,1)S(1)}, bf16[2,2,2,128,128]{4,3,2,1,0:T(8,128)(2,1)S(1)}, u32[]{:S(2)}, u32[]{:S(2)}) collective-permute-start(bf16[2,2,2,128,128]{4,3,2,1,0:T(8,128)(2,1)S(1)} %collective-permute-done.4.refs_6_), channel_id=1, source_target_pairs={{8,0},{12,4},{16,8},{20,12},{24,16},{28,20},{32,24},{36,28},{40,32... | collective-permute-start | bytes 786440 | tf_op jit(solution)/shard_map/ppermute | solution.py:257
  23.7 15.3 %collective-permute-start.2 = (bf16[2096,128]{1,0:T(8,128)(2,1)}, bf16[2096,128]{1,0:T(8,128)(2,1)S(1)}, u32[]{:S(2)}, u32[]{:S(2)}) collective-permute-start(bf16[2096,128]{1,0:T(8,128)(2,1)} %get-tuple-element.20.refs_2_), channel_id=1, source_target_pairs={{192,0},{196,4},{200,8},{204,12},{208,16},{212,20},{216,24},{220,2... | collective-permute-start | bytes 1609736 | tf_op jit(solution)/shard_map/ppermute | solution.py:257
  25.3 16.8 %collective-permute-start.1 = (bf16[2096,128]{1,0:T(8,128)(2,1)S(1)}, bf16[2096,128]{1,0:T(8,128)(2,1)S(1)}, u32[]{:S(2)}, u32[]{:S(2)}) collective-permute-start(bf16[2096,128]{1,0:T(8,128)(2,1)S(1)} %collective-permute-done.refs_3_), channel_id=1, source_target_pairs={{64,0},{68,4},{72,8},{76,12},{80,16},{84,20},{88,24},{92,28},{96,3... | collective-permute-start | bytes 1609736 | tf_op jit(solution)/shard_map/ppermute | solution.py:257
  27.0 7.6 %collective-permute-start.8 = (bf16[2,2,2,128,128]{4,3,2,1,0:T(8,128)(2,1)S(1)}, bf16[2,2,2,128,128]{4,3,2,1,0:T(8,128)(2,1)S(1)}, u32[]{:S(2)}, u32[]{:S(2)}) collective-permute-start(bf16[2,2,2,128,128]{4,3,2,1,0:T(8,128)(2,1)S(1)} %collective-permute-done.6.refs_7_), channel_id=1, source_target_pairs={{56,0},{60,4},{0,8},{4,12},{8,16},{12,20},{16,24},{20,28},{24,32},... | collective-permute-start | bytes 786440 | tf_op jit(solution)/shard_map/ppermute | solution.py:257
  27.6 7.7 %collective-permute-start.7 = (bf16[2,2,2,128,128]{4,3,2,1,0:T(8,128)(2,1)S(1)}, bf16[2,2,2,128,128]{4,3,2,1,0:T(8,128)(2,1)S(1)}, u32[]{:S(2)}, u32[]{:S(2)}) collective-permute-start(bf16[2,2,2,128,128]{4,3,2,1,0:T(8,128)(2,1)S(1)} %collective-permute-done.5.refs_6_), channel_id=1, source_target_pairs={{8,0},{12,4},{16,8},{20,12},{24,16},{28,20},{32,24},{36,28},{40,32... | collective-permute-start | bytes 786440 | tf_op jit(solution)/shard_map/ppermute | solution.py:257
  34.5 7.6 %collective-permute-start.10 = (bf16[2,2,2,128,128]{4,3,2,1,0:T(8,128)(2,1)S(1)}, bf16[2,2,2,128,128]{4,3,2,1,0:T(8,128)(2,1)S(1)}, u32[]{:S(2)}, u32[]{:S(2)}) collective-permute-start(bf16[2,2,2,128,128]{4,3,2,1,0:T(8,128)(2,1)S(1)} %collective-permute-done.8.refs_7_), channel_id=1, source_target_pairs={{56,0},{60,4},{0,8},{4,12},{8,16},{12,20},{16,24},{20,28},{24,32},... | collective-permute-start | bytes 786440 | tf_op jit(solution)/shard_map/ppermute | solution.py:257
  35.3 7.6 %collective-permute-start.9 = (bf16[2,2,2,128,128]{4,3,2,1,0:T(8,128)(2,1)S(1)}, bf16[2,2,2,128,128]{4,3,2,1,0:T(8,128)(2,1)}, u32[]{:S(2)}, u32[]{:S(2)}) collective-permute-start(bf16[2,2,2,128,128]{4,3,2,1,0:T(8,128)(2,1)S(1)} %collective-permute-done.7.refs_6_), channel_id=1, source_target_pairs={{8,0},{12,4},{16,8},{20,12},{24,16},{28,20},{32,24},{36,28},{40,32... | collective-permute-start | bytes 786440 | tf_op jit(solution)/shard_map/ppermute | solution.py:257
  42.9 1.0 %copy-start = (bf16[2096,128]{1,0:T(8,128)(2,1)S(1)}, bf16[2096,128]{1,0:T(8,128)(2,1)}, u32[]{:S(2)}) copy-start(bf16[2096,128]{1,0:T(8,128)(2,1)} %get-tuple-element.20.refs_2_) | copy-start | bytes 1609732
  43.9 0.7 copy-start.1
  53.3 20.8 %collective-permute-start.14 = (bf16[2,256,256]{2,1,0:T(8,128)(2,1)S(1)}, bf16[2,256,256]{2,1,0:T(8,128)(2,1)S(1)}, u32[]{:S(2)}, u32[]{:S(2)}) collective-permute-start(bf16[2,256,256]{2,1,0:T(8,128)(2,1)S(1)} %get-tuple-element.32), channel_id=1, source_target_pairs={{8,0},{12,4},{16,8},{20,12},{24,16},{28,20},{32,24},{36,28},{40,32... | collective-permute-start | bytes 786440 | tf_op jit(solution)/shard_map/ppermute | solution.py:257
  57.4 8.3 %collective-permute-start.17 = (bf16[2,256,256]{2,1,0:T(8,128)(2,1)S(1)}, bf16[2,256,256]{2,1,0:T(8,128)(2,1)S(1)}, u32[]{:S(2)}, u32[]{:S(2)}) collective-permute-start(bf16[2,256,256]{2,1,0:T(8,128)(2,1)S(1)} %get-tuple-element.36), channel_id=1, source_target_pairs={{56,0},{60,4},{0,8},{4,12},{8,16},{12,20},{16,24},{20,28},{24,32},... | collective-permute-start | bytes 786440 | tf_op jit(solution)/shard_map/ppermute | solution.py:257
  65.7 11.8 %collective-permute-start.18 = (bf16[2,256,256]{2,1,0:T(8,128)(2,1)S(1)}, bf16[2,256,256]{2,1,0:T(8,128)(2,1)S(1)}, u32[]{:S(2)}, u32[]{:S(2)}) collective-permute-start(bf16[2,256,256]{2,1,0:T(8,128)(2,1)S(1)} %add_convert_fusion.2), channel_id=1, source_target_pairs={{56,0},{60,4},{0,8},{4,12},{8,16},{12,20},{16,24},{20,28},{24,32},... | collective-permute-start | bytes 786440 | tf_op jit(solution)/shard_map/ppermute | solution.py:257
  74.2 12.4 %collective-permute-start.15 = (bf16[2,256,256]{2,1,0:T(8,128)(2,1)S(1)}, bf16[2,256,256]{2,1,0:T(8,128)(2,1)S(1)}, u32[]{:S(2)}, u32[]{:S(2)}) collective-permute-start(bf16[2,256,256]{2,1,0:T(8,128)(2,1)S(1)} %add_convert_fusion.4), channel_id=1, source_target_pairs={{8,0},{12,4},{16,8},{20,12},{24,16},{28,20},{32,24},{36,28},{40,32... | collective-permute-start | bytes 786440 | tf_op jit(solution)/shard_map/ppermute | solution.py:257
  77.6 12.4 %collective-permute-start.19 = (bf16[2,256,256]{2,1,0:T(8,128)(2,1)S(1)}, bf16[2,256,256]{2,1,0:T(8,128)(2,1)S(1)}, u32[]{:S(2)}, u32[]{:S(2)}) collective-permute-start(bf16[2,256,256]{2,1,0:T(8,128)(2,1)S(1)} %add_convert_fusion.1), channel_id=1, source_target_pairs={{56,0},{60,4},{0,8},{4,12},{8,16},{12,20},{16,24},{20,28},{24,32},... | collective-permute-start | bytes 786440 | tf_op jit(solution)/shard_map/ppermute | solution.py:257
  86.7 9.8 %collective-permute-start.16 = (bf16[2,256,256]{2,1,0:T(8,128)(2,1)S(1)}, bf16[2,256,256]{2,1,0:T(8,128)(2,1)S(1)}, u32[]{:S(2)}, u32[]{:S(2)}) collective-permute-start(bf16[2,256,256]{2,1,0:T(8,128)(2,1)S(1)} %add_convert_fusion.3), channel_id=1, source_target_pairs={{8,0},{12,4},{16,8},{20,12},{24,16},{28,20},{32,24},{36,28},{40,32... | collective-permute-start | bytes 786440 | tf_op jit(solution)/shard_map/ppermute | solution.py:257
  90.0 7.7 %collective-permute-start.20 = (bf16[2,256,256]{2,1,0:T(8,128)(2,1)S(1)}, bf16[2,256,256]{2,1,0:T(8,128)(2,1)S(1)}, u32[]{:S(2)}, u32[]{:S(2)}) collective-permute-start(bf16[2,256,256]{2,1,0:T(8,128)(2,1)S(1)} %add_convert_fusion), channel_id=1, source_target_pairs={{56,0},{60,4},{0,8},{4,12},{8,16},{12,20},{16,24},{20,28},{24,32},... | collective-permute-start | bytes 786440 | tf_op jit(solution)/shard_map/ppermute | solution.py:257
  90.1 8.9 %collective-permute-start.11 = (bf16[256,512]{1,0:T(8,128)(2,1)S(1)}, bf16[256,512]{1,0:T(8,128)(2,1)S(1)}, u32[]{:S(2)}, u32[]{:S(2)}) collective-permute-start(bf16[256,512]{1,0:T(8,128)(2,1)S(1)} %get-tuple-element.26), channel_id=1, source_target_pairs={{192,0},{196,4},{200,8},{204,12},{208,16},{212,20},{216,24},{220,2... | collective-permute-start | bytes 786440 | tf_op jit(solution)/shard_map/ppermute | solution.py:257
  92.2 9.6 %collective-permute-start.12 = (bf16[256,512]{1,0:T(8,128)(2,1)S(1)}, bf16[256,512]{1,0:T(8,128)(2,1)S(1)}, u32[]{:S(2)}, u32[]{:S(2)}) collective-permute-start(bf16[256,512]{1,0:T(8,128)(2,1)S(1)} %get-tuple-element.27), channel_id=1, source_target_pairs={{128,0},{132,4},{136,8},{140,12},{144,16},{148,20},{152,24},{156,2... | collective-permute-start | bytes 786440 | tf_op jit(solution)/shard_map/ppermute | solution.py:257
  94.7 7.2 %collective-permute-start.13 = (bf16[256,512]{1,0:T(8,128)(2,1)S(1)}, bf16[256,512]{1,0:T(8,128)(2,1)S(1)}, u32[]{:S(2)}, u32[]{:S(2)}) collective-permute-start(bf16[256,512]{1,0:T(8,128)(2,1)S(1)} %get-tuple-element.28), channel_id=1, source_target_pairs={{64,0},{68,4},{72,8},{76,12},{80,16},{84,20},{88,24},{92,28},{96,3... | collective-permute-start | bytes 786440 | tf_op jit(solution)/shard_map/ppermute | solution.py:257
  97.8 5.1 %collective-permute-start.21 = (bf16[256,256]{1,0:T(8,128)(2,1)S(1)}, bf16[256,256]{1,0:T(8,128)(2,1)S(1)}, u32[]{:S(2)}, u32[]{:S(2)}) collective-permute-start(bf16[256,256]{1,0:T(8,128)(2,1)S(1)} %fusion.1), channel_id=1, source_target_pairs={{4,0},{0,4},{12,8},{8,12},{20,16},{16,20},{28,24},{24,28},{36,32},... | collective-permute-start | bytes 393224 | tf_op jit(solution)/shard_map/ppermute | solution.py:257
